TPU v7x, 32 devices: a whole 2x2x4 slice. The times are simulated.
32 devices in a mesh: dp: 2 (over core), mp: 4 (over y, x), hidden: 4 (over z).
Axes of the slice: x: 2, y: 2, z: 4, core: 2. Of those that a mesh axis runs over, the one named last changes fastest.
Arguments:
- tokens: bfloat16 [1024, 8192], P('dp', 'mp'), may hold values from -6 to 6
- out_grad: bfloat16 [1024, 8192], P('dp', 'mp'), may hold values from -6 to 6
- gate_weight: bfloat16 [8192, 14336], P('mp', 'hidden'), may hold values from -0.0625 to 0.0625
- up_weight: bfloat16 [8192, 14336], P('mp', 'hidden'), may hold values from -0.0625 to 0.0625
- down_weight: bfloat16 [14336, 8192], P('hidden', 'mp'), may hold values from -0.046875 to 0.046875
- gate_keep: int32 [64, 112], P('mp', 'hidden'), may hold values from 0 to 1, as said below
- up_keep: int32 [64, 112], P('mp', 'hidden'), may hold values from 0 to 1, as said below
- down_keep: int32 [112, 64], P('hidden', 'mp'), may hold values from 0 to 1, as said below
- hidden_order: int32 [112], replicated, may hold values from 0 to 111, as said below
Outputs:
- gate_grad: bfloat16 [8192, 14336], P('mp', 'hidden')
- up_grad: bfloat16 [8192, 14336], P('mp', 'hidden')
- down_grad: bfloat16 [14336, 8192], P('hidden', 'mp')
Inputs may be any that keep to these rules, and one draw needn't show every extreme that they name: `gate_keep`: each block is kept or not; the share kept differs from one hidden block to another. `up_keep`: each block is kept or not; the share kept differs from one hidden block to another. `down_keep`: each block is kept or not; the share kept differs from one hidden block to another. `hidden_order`: A permutation of the hidden blocks. Of the 28 entries in each aligned group of 28 (the row blocks of down_weight on one index of hidden), at most 7 name hidden blocks in any one aligned group of 28 hidden blocks (the gate columns of one index of hidden), and some group reaches 7.
All inputs are finite; a program needn't handle non-finite values.
Results may differ from a plain program's by a relative error of at most 0.0067.
Values may be sent and summed in bfloat16 or wider, within the bound.
A program may use at most 320 MiB of HBM per device.

v0:
```python
import jax
import jax.numpy as jnp
from jax import lax
from jax.sharding import PartitionSpec as P

BLK = 128


def spread(keep):
    return jnp.repeat(jnp.repeat(keep.astype(jnp.bfloat16), BLK, 0), BLK, 1)


def group_terms(tok_rows, grad_rows, moved_rows, gate_rows, up_rows, gate_mask, up_mask, down_mask):
    gate_term = (
        jnp.einsum("td,tf->df", tok_rows, gate_rows, preferred_element_type=jnp.float32) * gate_mask
    ).astype(jnp.bfloat16)
    up_term = (
        jnp.einsum("td,tf->df", tok_rows, up_rows, preferred_element_type=jnp.float32) * up_mask
    ).astype(jnp.bfloat16)
    down_term = (
        jnp.einsum("tf,td->fd", moved_rows, grad_rows, preferred_element_type=jnp.float32)
        * down_mask
    ).astype(jnp.bfloat16)
    return (gate_term, up_term, down_term)


def shards(
    tokens,
    out_grad,
    gate_weight,
    up_weight,
    down_weight,
    gate_keep,
    up_keep,
    down_keep,
    hidden_order,
):
    here = lax.axis_index("hidden")
    blocks_dev = gate_weight.shape[1] // BLK
    gate_mask = spread(gate_keep)
    up_mask = spread(up_keep)
    down_mask = spread(down_keep)
    gate_part = jnp.dot(tokens, gate_weight * gate_mask, preferred_element_type=jnp.float32)
    up_part = jnp.dot(tokens, up_weight * up_mask, preferred_element_type=jnp.float32)
    gate, up = lax.psum((gate_part, up_part), "mp")
    sig = jax.nn.sigmoid(gate)
    act = gate * sig
    hidden_act = (act * up).astype(jnp.bfloat16)
    rows = hidden_act.shape[0]
    whole = lax.all_gather(hidden_act, "hidden", axis=1, tiled=True)
    held = lax.dynamic_slice_in_dim(hidden_order, here * blocks_dev, blocks_dev)
    moved = jnp.take(whole.reshape(rows, -1, BLK), held, axis=1).reshape(rows, -1)
    grad_part = jnp.einsum(
        "td,fd->tf", out_grad, down_weight * down_mask, preferred_element_type=jnp.float32
    )
    grad_sum = lax.psum(grad_part, "mp")
    grad_held = grad_sum.astype(jnp.bfloat16)
    every = lax.all_gather(grad_held, "hidden", axis=1, tiled=True)
    total_blocks = hidden_order.shape[0]
    wanted = here * blocks_dev + jnp.arange(blocks_dev, dtype=jnp.int32)
    stored = jnp.sum(
        jnp.where(
            hidden_order[None, :] == wanted[:, None],
            jnp.arange(total_blocks, dtype=jnp.int32)[None, :],
            0,
        ),
        axis=1,
    )
    hidden_grad = jnp.take(every.reshape(rows, -1, BLK), stored, axis=1).reshape(rows, -1)
    gate_delta = (hidden_grad * up * (sig * (1.0 + gate * (1.0 - sig)))).astype(jnp.bfloat16)
    up_delta = (hidden_grad * act).astype(jnp.bfloat16)
    gate_term, up_term, down_term = group_terms(
        tokens, out_grad, moved, gate_delta, up_delta, gate_mask, up_mask, down_mask
    )
    gate_sum, up_sum, down_sum = (
        lax.psum(gate_term, "dp").astype(jnp.float32),
        lax.psum(up_term, "dp").astype(jnp.float32),
        lax.psum(down_term, "dp").astype(jnp.float32),
    )
    return (
        gate_sum.astype(jnp.bfloat16),
        up_sum.astype(jnp.bfloat16),
        down_sum.astype(jnp.bfloat16),
    )


def solution(mesh):
    placed = (
        P("dp", "mp"),
        P("dp", "mp"),
        P("mp", "hidden"),
        P("mp", "hidden"),
        P("hidden", "mp"),
        P("mp", "hidden"),
        P("mp", "hidden"),
        P("hidden", "mp"),
        P(),
    )
    return jax.shard_map(
        shards,
        mesh=mesh,
        in_specs=placed,
        out_specs=(P("mp", "hidden"), P("mp", "hidden"), P("hidden", "mp")),
        check_vma=False,
    )
```

profile of v0, /device:TPU:0, one launch (start us, length us, event | category | flops | bytes accessed | tf_op | source)
XLA Modules:
  0.0 1299.4 jit_solution(8126292703363366205)
XLA Ops:
  8.0 0.0 copy-start
  8.0 0.0 all-reduce.6.cloned.1.call-start
  8.1 0.8 convert_element_type.57
  8.9 0.1 copy.22
  9.0 0.7 convert_element_type.56
  9.7 0.1 copy.20
  9.8 0.1 broadcast_bitcast_fusion.1
  10.0 0.1 broadcast_bitcast_fusion
  10.2 20.2 %copy.23 = bf16[2048,3584]{0,1:T(8,128)(2,1)} copy(bf16[2048,3584]{1,0:T(8,128)(2,1)} %param.13) | data formatting | bytes 29360128 | tf_op args[2]
  30.4 20.2 %copy.21 = bf16[2048,3584]{0,1:T(8,128)(2,1)} copy(bf16[2048,3584]{1,0:T(8,128)(2,1)} %param.14) | data formatting | bytes 29360128 | tf_op args[3]
  50.7 14.5 %bitcast_multiply_fusion.2 = bf16[2048,3584]{0,1:T(8,128)(2,1)} fusion(bf16[2048,3584]{0,1:T(8,128)(2,1)} %copy.23, bf16[2048,28]{0,1:T(8,128)(2,1)S(1)} %bitcast.68), kind=kLoop, calls=%fused_computation.7 | loop fusion | flops 7340032 | bytes 29474816 | tf_op jit(solution)/shard_map/mul | solution.py:43
  65.2 13.1 %convolution_bitcast_fusion = f32[512,3584]{0,1:T(8,128)} fusion(bf16[2048,3584]{0,1:T(8,128)(2,1)} %bitcast_multiply_fusion.2, bf16[512,2048]{1,0:T(8,128)(2,1)S(1)} %copy-done), kind=kOutput, calls=%fused_computation.20 | convolution fusion | flops 7516192768 | bytes 24117248 | tf_op jit(solution)/shard_map/dot_general | solution.py:43
  78.3 0.0 slice-done.2
  78.3 0.0 slice-done.3
  78.3 5.9 bitcast_multiply_fusion.3
  84.3 13.0 convolution_bitcast_fusion.1
  97.2 0.0 all-reduce.6.cloned.1.call-update
  97.3 0.2 all-gather.3.cloned.1.call-start
  97.5 0.4 copy-done.1
  97.9 0.1 copy.19
  98.0 0.1 broadcast_in_dim.42
  98.2 0.0 copy-start.3
  98.2 9.8 broadcast_in_dim.43
  108.0 0.0 copy-done.3
  108.0 15.7 %fusion.8 = f32[512,3584]{0,1:T(8,128)} fusion(bf16[512,2048]{1,0:T(8,128)(2,1)S(1)} %copy-done.3, bf16[3584,2048]{1,0:T(8,128)(2,1)} %param.15, bf16[448,8,16,128]{3,2,1,0:T(8,128)(2,1)} %bitcast.62), kind=kOutput, calls=%fused_computation.22 | convolution fusion | flops 7523532800 | bytes 38797312 | tf_op jit(solution)/shard_map/td,fd->tf/dot_general | solution.py:53
  123.7 455.7 %all-reduce.9 = bf16[512,3584]{0,1:T(8,128)(2,1)} all-reduce(f32[512,3584]{0,1:T(8,128)} %fusion.8), channel_id=1, replica_groups=mesh['dp'=2,'mp'=4,'hidden'=4] {'mp'}, use_global_device_ids=true, to_apply=%region_0.0 | all-reduce | flops 1835008 | bytes 11010048 | tf_op jit(solution)/shard_map/psum | solution.py:56
  579.4 0.0 all-gather.3.cloned.1.call-update
  579.5 0.0 all-gather.5.cloned.1.call-start
  579.5 0.9 all-reduce.6.cloned.1.call-done
  580.4 7.7 multiply_convert_fusion.1
  588.1 0.0 all-gather.5.cloned.1.call-update
  588.1 0.3 all-reduce.8.cloned.1.call-start
  588.4 0.1 compare_and_fusion
  588.5 0.2 select_reduce_fusion
  588.7 243.2 %all-gather.3.cloned.1.call-done = bf16[512,14336]{0,1:T(8,128)(2,1)} async-done(((bf16[512,3584]{0,1:T(8,128)(2,1)}), bf16[512,14336]{0,1:T(8,128)(2,1)}) %all-gather.3.cloned.1.call-update) | async-done | bytes 14680080 | tf_op jit(solution)/shard_map/all_gather | solution.py:58
  831.9 7.9 gather_fusion
  839.8 4.9 broadcast_select_fusion.1
  844.7 21.4 %fusion.1 = bf16[2048,3584]{0,1:T(8,128)(2,1)} fusion(bf16[512,2048]{1,0:T(8,128)(2,1)S(1)} %copy-done, bf16[2048,28]{0,1:T(8,128)(2,1)S(1)} %bitcast.69, f32[512,3584]{0,1:T(8,128)} %get-tuple-element.10, bf16[512,3584]{0,1:T(8,128)(2,1)} %bitcast.60, f32[512,3584]{0,1:T(8,128)} %get-tuple-element.11), kind=kOutput, calls=%fused_computation.5 | convolution fusion | flops 7558397952 | bytes 35241984 | tf_op jit(solution)/shard_map/td,tf->df/dot_general | solution.py:15
  866.1 16.4 %fusion = bf16[2048,3584]{0,1:T(8,128)(2,1)} fusion(bf16[512,2048]{1,0:T(8,128)(2,1)S(1)} %copy-done, bf16[2048,28]{0,1:T(8,128)(2,1)S(1)} %bitcast.71, bf16[512,3584]{0,1:T(8,128)(2,1)} %bitcast.61, f32[512,3584]{0,1:T(8,128)} %get-tuple-element.11), kind=kOutput, calls=%fused_computation.3 | convolution fusion | flops 7551057920 | bytes 27901952 | tf_op jit(solution)/shard_map/td,tf->df/dot_general | solution.py:18
  882.5 201.4 %all-gather.5.cloned.1.call-done = bf16[512,14336]{0,1:T(8,128)(2,1)} async-done(((bf16[512,3584]{0,1:T(8,128)(2,1)}), bf16[512,14336]{0,1:T(8,128)(2,1)}) %all-gather.5.cloned.1.call-update) | async-done | bytes 14680080 | tf_op jit(solution)/shard_map/all_gather | solution.py:50
  1083.9 7.8 gather_fusion.1
  1091.7 4.3 broadcast_select_fusion
  1096.0 16.3 %multiply_convert_fusion = bf16[3584,2048]{1,0:T(8,128)(2,1)} fusion(bf16[512,3584]{0,1:T(8,128)(2,1)} %bitcast.64, bf16[512,2048]{1,0:T(8,128)(2,1)} %param.12, bf16[448,8,16,128]{3,2,1,0:T(8,128)(2,1)} %bitcast.63), kind=kOutput, calls=%fused_computation.6 | convolution fusion | flops 7538212864 | bytes 35127296 | tf_op jit(solution)/shard_map/tf,td->fd/dot_general | solution.py:21
  1112.3 0.0 all-reduce.8.cloned.1.call-update
  1112.4 128.9 %all-reduce.8.cloned.1.call-done = (bf16[2048,3584]{0,1:T(8,128)(2,1)}, bf16[2048,3584]{0,1:T(8,128)(2,1)}, bf16[3584,2048]{1,0:T(8,128)(2,1)}) async-done(((bf16[2048,3584]{0,1:T(8,128)(2,1)}, bf16[2048,3584]{0,1:T(8,128)(2,1)}, bf16[3584,2048]{1,0:T(8,128)(2,1)}), (bf16[2048,3584]{0,1:T(8,128)(2,1)}, bf16[2048,3584]{0,1:T(8,128)(2,1)}, bf16[3584,2048]{1,0:T(8,128)(2,1)})) %all-reduce.8.cloned.1.call-update) | async-done | bytes 44040208 | tf_op jit(solution)/shard_map/psum | solution.py:76
  1241.3 18.6 %copy.24 = bf16[2048,3584]{1,0:T(8,128)(2,1)} copy(bf16[2048,3584]{0,1:T(8,128)(2,1)} %get-tuple-element.12) | data formatting | bytes 29360128
  1259.9 18.6 %copy.25 = bf16[2048,3584]{1,0:T(8,128)(2,1)} copy(bf16[2048,3584]{0,1:T(8,128)(2,1)} %get-tuple-element.13) | data formatting | bytes 29360128
  1278.5 13.5 %copy.43 = bf16[3584,2048]{1,0:T(8,128)(2,1)} copy(bf16[3584,2048]{1,0:T(8,128)(2,1)} %get-tuple-element.19) | data formatting | bytes 29360128
  (21 shorter events, 0.2 us)
Async XLA Ops:
  8.0 57.2 %copy-start = (bf16[512,2048]{1,0:T(8,128)(2,1)S(1)}, bf16[512,2048]{1,0:T(8,128)(2,1)}, u32[]{:S(2)}) copy-start(bf16[512,2048]{1,0:T(8,128)(2,1)} %param.11) | copy-start | bytes 6291460
  8.0 572.4 %all-reduce.6.cloned.1.call-start = ((), (), s32[]{:S(2)}) async-start(), calls=%async_computation.2 | async-start | bytes 29360128 | tf_op jit(solution)/shard_map/psum | solution.py:45
  50.7 27.6 %slice-start = ((s8[14680064]{0:T(1024)(128)(4,1)}), s8[4194304]{0:T(1024)(128)(4,1)S(1)}, s32[]{:S(2)}) async-start(s8[14680064]{0:T(1024)(128)(4,1)} %bitcast.58), calls=%async_computation.4 | async-start | bytes 8388608
  50.7 27.6 %slice-start.1 = ((s8[14680064]{0:T(1024)(128)(4,1)}), s8[4194304]{0:T(1024)(128)(4,1)S(1)}, s32[]{:S(2)}) async-start(s8[14680064]{0:T(1024)(128)(4,1)} %bitcast.58), calls=%async_computation.5 | async-start | bytes 8388608
  65.2 13.1 %slice-start.2 = ((s8[14680064]{0:T(1024)(128)(4,1)}), s8[4194304]{0:T(1024)(128)(4,1)S(1)}, s32[]{:S(2)}) async-start(s8[14680064]{0:T(1024)(128)(4,1)} %bitcast.58), calls=%async_computation.6 | async-start | bytes 8388608
  65.2 13.1 %slice-start.3 = ((s8[14680064]{0:T(1024)(128)(4,1)}), s8[2097152]{0:T(1024)(128)(4,1)S(1)}, s32[]{:S(2)}) async-start(s8[14680064]{0:T(1024)(128)(4,1)} %bitcast.58), calls=%async_computation.7 | async-start | bytes 4194304
  97.2 0.7 copy-start.1
  97.3 734.7 %all-gather.3.cloned.1.call-start = ((), (), s32[]{:S(2)}) async-start(), calls=%async_computation | async-start | bytes 18350080 | tf_op jit(solution)/shard_map/all_gather | solution.py:58
  98.2 9.9 copy-start.3
  579.5 504.4 %all-gather.5.cloned.1.call-start = ((), (), s32[]{:S(2)}) async-start(), calls=%async_computation.1 | async-start | bytes 18350080 | tf_op jit(solution)/shard_map/all_gather | solution.py:50
  580.4 8.0 copy-start.2
  588.1 653.2 %all-reduce.8.cloned.1.call-start = ((), (), s32[]{:S(2)}) async-start(), calls=%async_computation.3 | async-start | bytes 88080384 | tf_op jit(solution)/shard_map/psum | solution.py:76
Sparse Core Ops, SparseCore 0:
  97.4 482.9 all-reduce.5
  1112.5 128.7 all-reduce.7
Sparse Core Ops, SparseCore 1:
  579.5 252.3 all-gather.2
  833.3 250.5 all-gather.4
where the time goes:
time: 1300 us
  waiting for transfers between devices  574 us (44%)
  blocking collectives  456 us (35%)
  local copies, waits for them, and re-layouts  118 us (9%)
  matrix products  96 us (7%)
  other arithmetic  39.2 us (3%)
  between operations  15.6 us (1%)
    psum x1, blocking collectives, shards(): grad_sum = lax.psum(grad_part, 'mp')  456 us
    all_gather x1, waiting for transfers between devices, shards(): every = lax.all_gather(grad_held, 'hidden', axis=1, tiled=True)  243 us
    all_gather x1, waiting for transfers between devices, shards(): whole = lax.all_gather(hidden_act, 'hidden', axis=1, tiled=True)  201 us
    psum x1, waiting for transfers between devices, shards(): lax.psum(gate_term, 'dp').astype(jnp.float32)  129 us
    unnamed x27, local copies, waits for them, and re-layouts  92 us
  transfers between devices with their start and end apart: 4, of which 4 were waited for; matrix products, arithmetic and copies ran while one was open for 6% of the time, Pallas kernels for 0%

commit v1 on v0

v1 whole, which is shorter than its diff:
```python
import functools

import jax
import jax.numpy as jnp
from jax import lax
from jax.experimental import pallas as pl
from jax.experimental.pallas import tpu as pltpu
from jax.sharding import PartitionSpec as P

BLK = 128
F32 = jnp.float32
BF16 = jnp.bfloat16
NN = (((1,), (0,)), ((), ()))
NT = (((1,), (1,)), ((), ()))
TN = (((0,), (0,)), ((), ()))
VMEM_LIMIT = 48 * 1024 * 1024


def tile_blocks(blocks):
    return max(t for t in (1, 2, 4) if blocks % t == 0)


def params():
    return pltpu.CompilerParams(vmem_limit_bytes=VMEM_LIMIT)


def cost(rows, inner, cols, nbytes):
    return pl.CostEstimate(flops=2 * rows * inner * cols, bytes_accessed=nbytes, transcendentals=0)


def masked_into(dst, src, keep, row0, col0):
    rows, cols = src.shape
    for i in range(rows // BLK):
        for j in range(cols // BLK):
            at = (slice(i * BLK, (i + 1) * BLK), slice(j * BLK, (j + 1) * BLK))
            block = src[at]
            dst[at] = jnp.where(keep[row0 + i, col0 + j] != 0, block, jnp.zeros_like(block))


def columns_kernel(tb, keep, x, w, out, held):
    masked_into(held, w, keep, 0, pl.program_id(0) * tb)
    out[...] = lax.dot_general(x[...], held[...], NN, preferred_element_type=F32).astype(BF16)


def rows_kernel(tb, keep, x, w, out, held):
    masked_into(held, w, keep, pl.program_id(0) * tb, 0)
    out[...] = lax.dot_general(x[...], held[...], NT, preferred_element_type=F32).astype(BF16)


def times_columns(x, w, keep):
    rows, depth = x.shape
    cols = w.shape[1]
    tb = tile_blocks(cols // BLK)
    tn = tb * BLK
    return pl.pallas_call(
        functools.partial(columns_kernel, tb),
        grid=(cols // tn,),
        out_shape=jax.ShapeDtypeStruct((rows, cols), BF16),
        in_specs=[
            pl.BlockSpec(memory_space=pltpu.SMEM),
            pl.BlockSpec((rows, depth), lambda j: (0, 0)),
            pl.BlockSpec((depth, tn), lambda j: (0, j)),
        ],
        out_specs=pl.BlockSpec((rows, tn), lambda j: (0, j)),
        scratch_shapes=[pltpu.VMEM((depth, tn), BF16)],
        compiler_params=params(),
        cost_estimate=cost(rows, depth, cols, 2 * depth * cols + 2 * rows * cols),
    )(keep, x, w)


def times_rows(x, w, keep):
    rows, depth = x.shape
    cols = w.shape[0]
    tb = tile_blocks(cols // BLK)
    tn = tb * BLK
    return pl.pallas_call(
        functools.partial(rows_kernel, tb),
        grid=(cols // tn,),
        out_shape=jax.ShapeDtypeStruct((rows, cols), BF16),
        in_specs=[
            pl.BlockSpec(memory_space=pltpu.SMEM),
            pl.BlockSpec((rows, depth), lambda j: (0, 0)),
            pl.BlockSpec((tn, depth), lambda j: (j, 0)),
        ],
        out_specs=pl.BlockSpec((rows, tn), lambda j: (0, j)),
        scratch_shapes=[pltpu.VMEM((tn, depth), BF16)],
        compiler_params=params(),
        cost_estimate=cost(rows, depth, cols, 2 * depth * cols + 2 * rows * cols),
    )(keep, x, w)


def store_masked(out, value, keep, row0, col0, base):
    rows, cols = value.shape
    for i in range(rows // BLK):
        for j in range(cols // BLK):
            block = value[i * BLK : (i + 1) * BLK, j * BLK : (j + 1) * BLK]
            out[base + i * BLK : base + (i + 1) * BLK, j * BLK : (j + 1) * BLK] = jnp.where(
                keep[row0 + i, col0 + j] != 0, block, jnp.zeros_like(block)
            ).astype(BF16)


def in_grad_kernel(tb, strip, keep, xt, d0, d1, out):
    col0 = pl.program_id(0) * tb
    half = d0.shape[0]
    for base in range(0, xt.shape[0], strip):
        value = lax.dot_general(
            xt[base : base + strip, :half], d0[...], NN, preferred_element_type=F32
        ) + lax.dot_general(xt[base : base + strip, half:], d1[...], NN, preferred_element_type=F32)
        store_masked(out, value, keep, base // BLK, col0, base)


def in_grad(xt, d0, d1, keep):
    rows, depth = xt.shape
    half, cols = d0.shape
    tb = tile_blocks(cols // BLK)
    tn = tb * BLK
    return pl.pallas_call(
        functools.partial(in_grad_kernel, tb, min(512, rows)),
        grid=(cols // tn,),
        out_shape=jax.ShapeDtypeStruct((rows, cols), BF16),
        in_specs=[
            pl.BlockSpec(memory_space=pltpu.SMEM),
            pl.BlockSpec((rows, depth), lambda j: (0, 0)),
            pl.BlockSpec((half, tn), lambda j: (0, j)),
            pl.BlockSpec((half, tn), lambda j: (0, j)),
        ],
        out_specs=pl.BlockSpec((rows, tn), lambda j: (0, j)),
        compiler_params=params(),
        cost_estimate=cost(rows, depth, cols, 2 * depth * cols + 2 * rows * cols),
    )(keep, xt, d0, d1)


def out_grad_kernel(tb, keep, m0, m1, g0, g1, out):
    row0 = pl.program_id(0) * tb
    value = lax.dot_general(m0[...], g0[...], TN, preferred_element_type=F32) + lax.dot_general(
        m1[...], g1[...], TN, preferred_element_type=F32
    )
    store_masked(out, value, keep, row0, 0, 0)


def down_grad(m0, m1, g0, g1, keep):
    half, rows = m0.shape
    cols = g0.shape[1]
    tb = tile_blocks(rows // BLK)
    tm = tb * BLK
    return pl.pallas_call(
        functools.partial(out_grad_kernel, tb),
        grid=(rows // tm,),
        out_shape=jax.ShapeDtypeStruct((rows, cols), BF16),
        in_specs=[
            pl.BlockSpec(memory_space=pltpu.SMEM),
            pl.BlockSpec((half, tm), lambda j: (0, j)),
            pl.BlockSpec((half, tm), lambda j: (0, j)),
            pl.BlockSpec((half, cols), lambda j: (0, 0)),
            pl.BlockSpec((half, cols), lambda j: (0, 0)),
        ],
        out_specs=pl.BlockSpec((tm, cols), lambda j: (j, 0)),
        compiler_params=params(),
        cost_estimate=cost(rows, 2 * half, cols, 4 * half * rows + 2 * rows * cols),
    )(keep, m0, m1, g0, g1)


def swap(x, axis, n, bits):
    return lax.ppermute(x, axis, [(i, i ^ bits) for i in range(n)])


def mp_orders(n):
    up = [1 << b for b in range(n.bit_length() - 1)]
    return up, up[::-1]


def scatter_sum(part, n, me):
    rows, cols = part.shape
    levels = n.bit_length() - 1
    piece = rows // (2 * n)
    split = part.reshape(n, 2, piece, cols)
    halves = []
    for half, order in enumerate(mp_orders(n)):
        cur = split[:, half].reshape((2,) * levels + (piece, cols))
        left = list(range(levels))[::-1]
        for stride in order:
            bit = stride.bit_length() - 1
            axis = left.index(bit)
            mine = (me // stride) % 2
            sent = lax.dynamic_index_in_dim(cur, 1 - mine, axis, keepdims=False)
            kept = lax.dynamic_index_in_dim(cur, mine, axis, keepdims=False)
            got = swap(sent.astype(BF16), "mp", n, stride)
            cur = kept.astype(F32) + got.astype(F32)
            left.pop(axis)
        halves.append(cur.reshape(piece, cols))
    return jnp.concatenate(halves, 0)


def gather_tokens(own, n):
    piece = own.shape[0] // 2
    out = []
    for half, order in enumerate(mp_orders(n)):
        pieces = [own[half * piece : (half + 1) * piece]]
        for stride in order:
            pieces += [swap(p, "mp", n, stride) for p in pieces]
        out += pieces
    return jnp.concatenate(out, 0)


def gathered_order(x, n, me):
    piece = x.shape[0] // (2 * n)
    split = x.reshape(n, 2, piece, x.shape[1])
    out = []
    for half, order in enumerate(mp_orders(n)):
        offsets = [0]
        for stride in order:
            offsets += [o ^ stride for o in offsets]
        for o in offsets:
            out.append(lax.dynamic_index_in_dim(split[:, half], me ^ o, 0, keepdims=False))
    return jnp.concatenate(out, 0)


def to_blocks(x):
    return x.reshape(x.shape[0], -1, BLK).transpose(1, 0, 2)


def from_blocks(x):
    return x.transpose(1, 0, 2).reshape(x.shape[1], -1)


def exchange(blocks, picks, back, n, me):
    parts = []
    for s in range(n):
        part = jnp.take(blocks, lax.dynamic_index_in_dim(picks, me ^ s, 0, keepdims=False), axis=0)
        parts.append(part if s == 0 else swap(part, "hidden", n, s))
    return jnp.take(jnp.concatenate(parts, 0), back, axis=0)


def tables(hidden_order, n, me):
    per = hidden_order.shape[0] // n
    cap = -(-per // n)
    ids = hidden_order.reshape(n, per)
    src = ids // per
    k = jnp.arange(per, dtype=jnp.int32)
    same = src[:, :, None] == src[:, None, :]
    rank = jnp.sum(jnp.where(same & (k[None, None, :] < k[None, :, None]), 1, 0), axis=2)
    devs = jnp.arange(n, dtype=jnp.int32)
    slots = jnp.arange(cap, dtype=jnp.int32)
    my_src = lax.dynamic_index_in_dim(src, me, 0, keepdims=False)
    my_rank = lax.dynamic_index_in_dim(rank, me, 0, keepdims=False)
    stored_pick = jnp.sum(
        jnp.where(
            (my_src[None, None, :] == devs[:, None, None])
            & (my_rank[None, None, :] == slots[None, :, None]),
            k[None, None, :],
            0,
        ),
        axis=2,
    )
    hidden_pick = jnp.sum(
        jnp.where(
            (src[:, None, :] == me) & (rank[:, None, :] == slots[None, :, None]),
            (ids - me * per)[:, None, :],
            0,
        ),
        axis=2,
    )
    stored_back = (my_src ^ me) * cap + my_rank
    wanted = me * per + k
    hidden_back = jnp.sum(
        jnp.where(
            ids[None] == wanted[:, None, None],
            ((devs ^ me)[:, None] * cap + rank)[None],
            0,
        ),
        axis=(1, 2),
    )
    return stored_pick, stored_back, hidden_pick, hidden_back


def shards(n_dp, n_mp, n_hidden, tokens, out_grad, gate_weight, up_weight, down_weight, gate_keep, up_keep, down_keep, hidden_order):
    mp = lax.axis_index("mp")
    here = lax.axis_index("hidden")
    stored_pick, stored_back, hidden_pick, hidden_back = tables(hidden_order, n_hidden, here)

    grad_part = times_rows(out_grad, down_weight, down_keep)
    gate_part = times_columns(tokens, gate_weight, gate_keep)
    up_part = times_columns(tokens, up_weight, up_keep)

    grad_stored = scatter_sum(grad_part, n_mp, mp).astype(BF16)
    hidden_grad = from_blocks(
        exchange(to_blocks(grad_stored), stored_pick, hidden_back, n_hidden, here)
    )
    gate = scatter_sum(gate_part, n_mp, mp)
    up = scatter_sum(up_part, n_mp, mp)

    sig = jax.nn.sigmoid(gate)
    act = gate * sig
    hidden_act = (act * up).astype(BF16)
    moved = from_blocks(
        exchange(to_blocks(hidden_act), hidden_pick, stored_back, n_hidden, here)
    )
    hidden_grad = hidden_grad.astype(F32)
    gate_delta = (hidden_grad * up * (sig * (1.0 + gate * (1.0 - sig)))).astype(BF16)
    up_delta = (hidden_grad * act).astype(BF16)

    tok = gathered_order(tokens, n_mp, mp)
    grd = gathered_order(out_grad, n_mp, mp)
    tok_t = jnp.concatenate([tok, swap(tok, "dp", n_dp, 1)], 0).T
    grd_other = swap(grd, "dp", n_dp, 1)

    gate_all = gather_tokens(gate_delta, n_mp)
    gate_grad = in_grad(tok_t, gate_all, swap(gate_all, "dp", n_dp, 1), gate_keep)
    up_all = gather_tokens(up_delta, n_mp)
    up_grad = in_grad(tok_t, up_all, swap(up_all, "dp", n_dp, 1), up_keep)
    moved_all = gather_tokens(moved, n_mp)
    down = down_grad(moved_all, swap(moved_all, "dp", n_dp, 1), grd, grd_other, down_keep)
    return gate_grad, up_grad, down


def solution(mesh):
    placed = (
        P("dp", "mp"),
        P("dp", "mp"),
        P("mp", "hidden"),
        P("mp", "hidden"),
        P("hidden", "mp"),
        P("mp", "hidden"),
        P("mp", "hidden"),
        P("hidden", "mp"),
        P(),
    )
    sizes = (mesh.shape["dp"], mesh.shape["mp"], mesh.shape["hidden"])
    return jax.shard_map(
        functools.partial(shards, *sizes),
        mesh=mesh,
        in_specs=placed,
        out_specs=(P("mp", "hidden"), P("mp", "hidden"), P("hidden", "mp")),
        check_vma=False,
    )
```

time: 1300 us -> 392 us (0.30)
  waiting for transfers between devices: 574 us -> 108 us
  blocking collectives: 456 us -> 0 us
  Pallas kernels: 0 us -> 98.7 us
  matrix products: 96 us -> 0 us
  starting transfers between devices: 0.57 us -> 42.3 us
  local copies, waits for them, and re-layouts: 118 us -> 102 us
  between operations: 15.6 us -> 1.51 us
    psum x1 -> x0, blocking collectives: 456 us -> none  [shards(): grad_sum = lax.psum(grad_part, 'mp')]
    all_gather x2 -> x0, waiting for transfers between devices: 445 us -> none  [the longest x1 243 us: shards(): every = lax.all_gather(grad_held, 'hidden', axis=1, tiled=True)]
    psum x2 -> x0, waiting for transfers between devices: 130 us -> none  [the longest x1 129 us: shards(): lax.psum(gate_term, 'dp').astype(jnp.float32)]
    ppermute x0 -> x41, waiting for transfers between devices: none -> 108 us  [swap(): return lax.ppermute(x, axis, [(i, i ^ bits) for i in range(n)])]
    pallas_call x0 -> x6, Pallas kernels: none -> 98.7 us  [the longest x2 41.1 us: in_grad(): pl.pallas_call(functools.partial(in_grad_kernel, tb, min(512, rows)), gri...]
    dot_general x6 -> x0, matrix products: 96 us -> none  [the longest x1 21.4 us: group_terms(): jnp.einsum('td,tf->df', tok_rows, gate_rows, preferred_element_type=jnp.f...]
    unnamed x27 -> x123, local copies, waits for them, and re-layouts: 92 us -> 34.3 us
    ppermute x0 -> x41, starting transfers between devices: none -> 42.3 us  [swap(): return lax.ppermute(x, axis, [(i, i ^ bits) for i in range(n)])]
  transfers between devices with their start and end apart: 4 -> 41, of which waited for: 4 -> 14; matrix products, arithmetic and copies ran while one was open for 6% -> 30% of each run, Pallas kernels for 0% -> 20%
where the time goes in v1:
time: 392 us; the launch traced here: 390 us
  waiting for transfers between devices  108 us (28%)
  local copies, waits for them, and re-layouts  102 us (26%)
  Pallas kernels  98.7 us (25%)
  starting transfers between devices  42.3 us (11%)
  other arithmetic  37.7 us (10%)
    ppermute x41, waiting for transfers between devices, swap(): return lax.ppermute(x, axis, [(i, i ^ bits) for i in range(n)])  108 us
    ppermute x41, starting transfers between devices, swap(): return lax.ppermute(x, axis, [(i, i ^ bits) for i in range(n)])  42.3 us
    pallas_call x2, Pallas kernels, in_grad(): pl.pallas_call(functools.partial(in_grad_kernel, tb, min(512, rows)), gri...  41.1 us
    unnamed x123, local copies, waits for them, and re-layouts  34.3 us
    pallas_call x2, Pallas kernels, times_columns(): pl.pallas_call(functools.partial(columns_kernel, tb), grid=(cols // tn,),...  24.8 us
    pallas_call x1, Pallas kernels, down_grad(): pl.pallas_call(functools.partial(out_grad_kernel, tb), grid=(rows // tm,)...  20.3 us
    gather x8, local copies, waits for them, and re-layouts, exchange(): jnp.take(blocks, lax.dynamic_index_in_dim(picks, me ^ s, 0, keepdims=Fals...  13.5 us
    pallas_call x1, Pallas kernels, times_rows(): pl.pallas_call(functools.partial(rows_kernel, tb), grid=(cols // tn,), ou...  12.5 us
  transfers between devices with their start and end apart: 41, of which 14 were waited for; matrix products, arithmetic and copies ran while one was open for 30% of the time, Pallas kernels for 20%

profile of v1, /device:TPU:0, one launch (start us, length us, event | category | flops | bytes accessed | tf_op | source)
XLA Modules:
  0.0 389.6 jit_solution(15732048560481631520)
XLA Ops:
  0.6 1.7 fusion.30
  5.3 2.1 copy.143
  12.6 6.3 %concatenate.54 = bf16[512,2048]{0,1:T(8,128)(2,1)} concatenate(bf16[64,2048]{0,1:T(8,128)(2,1)} %bitcast.196, bf16[64,2048]{0,1:T(8,128)(2,1)} %bitcast.198, bf16[64,2048]{0,1:T(8,128)(2,1)} %bitcast.200, bf16[64,2048]{0,1:T(8,128)(2,1)} %bitcast.202, bf16[64,2048]{0,1:T(8,128)(2,1)} %bitcast.194, bf16[64,2048]{0,1:T(8,128)(2,1)} %bitcast.192, bf16[64,2048]{0,1:T(8,128)(2,1)S(1)} %bitcast.190, ...), dimensions={0} | concatenate | bytes 4194304 | tf_op jit(solution)/shard_map/concatenate | solution.py:215
  19.4 12.5 %shard_map.112 = bf16[512,3584]{1,0:T(8,128)(2,1)S(1)} custom-call(s32[28,16]{1,0:T(8,128)S(1)} %copy.115.keep, bf16[512,2048]{1,0:T(8,128)(2,1)S(1)} %copy-done, bf16[3584,2048]{1,0:T(8,128)(2,1)} %w.3), custom_call_target="tpu_custom_call" | custom-call | flops 7516192768 | bytes 18350080 | tf_op jit(solution)/shard_map/pallas_call | solution.py:76
  31.9 2.1 fusion.28
  35.2 2.6 collective-permute-start.1
  37.8 2.2 dynamic-slice_bitcast_fusion.4
  43.1 12.3 %shard_map.114 = bf16[512,3584]{1,0:T(8,128)(2,1)S(1)} custom-call(s32[16,28]{1,0:T(8,128)S(1)} %copy-done.3, bf16[512,2048]{1,0:T(8,128)(2,1)S(1)} %copy-done.1, bf16[2048,3584]{1,0:T(8,128)(2,1)} %w.5), custom_call_target="tpu_custom_call" | custom-call | flops 7516192768 | bytes 18350080 | tf_op jit(solution)/shard_map/pallas_call | solution.py:55
  68.4 12.5 %shard_map.113 = bf16[512,3584]{1,0:T(8,128)(2,1)S(1)} custom-call(s32[16,28]{1,0:T(8,128)S(1)} %copy-done.4, bf16[512,2048]{1,0:T(8,128)(2,1)S(1)} %copy-done.2, bf16[2048,3584]{1,0:T(8,128)(2,1)} %w.4), custom_call_target="tpu_custom_call" | custom-call | flops 7516192768 | bytes 18350080 | tf_op jit(solution)/shard_map/pallas_call | solution.py:55
  80.9 2.0 fusion.27
  92.4 2.0 convert_add_fusion.4
  97.3 11.6 %collective-permute-done.8 = bf16[2,64,3584]{2,1,0:T(8,128)(2,1)S(1)} collective-permute-done((bf16[2,64,3584]{2,1,0:T(8,128)(2,1)S(1)}, bf16[2,64,3584]{2,1,0:T(8,128)(2,1)S(1)}, u32[]{:S(2)}, u32[]{:S(2)}) %collective-permute-start.8) | collective-permute-done | bytes 917536 | tf_op jit(solution)/shard_map/ppermute | solution.py:164
  115.3 6.7 %collective-permute-done.2 = bf16[64,3584]{1,0:T(8,128)(2,1)S(1)} collective-permute-done((bf16[64,3584]{1,0:T(8,128)(2,1)S(1)}, bf16[64,3584]{1,0:T(8,128)(2,1)S(1)}, u32[]{:S(2)}, u32[]{:S(2)}) %collective-permute-start.2) | collective-permute-done | bytes 458784 | tf_op jit(solution)/shard_map/ppermute | solution.py:164
  128.2 1.9 broadcast_select_fusion.6
  130.1 1.8 collective-permute-done.13
  136.4 3.4 collective-permute-done.9
  146.2 2.4 gather_fusion.8
  148.7 2.4 gather_fusion.7
  151.1 2.5 gather_fusion.6
  153.5 2.4 gather_fusion.5
  159.8 2.6 collective-permute-start.31
  166.8 1.8 collective-permute-start.6
  168.5 16.8 %collective-permute-done.31 = bf16[7,128,128]{2,1,0:T(8,128)(2,1)S(1)} collective-permute-done((bf16[7,128,128]{2,1,0:T(8,128)(2,1)S(1)}, bf16[7,128,128]{2,1,0:T(8,128)(2,1)S(1)}, u32[]{:S(2)}, u32[]{:S(2)}) %collective-permute-start.31) | collective-permute-done | bytes 229408 | tf_op jit(solution)/shard_map/ppermute | solution.py:164
  186.5 2.8 gather_fusion.9
  194.8 2.9 collective-permute-done.6
  200.2 2.2 pad_maximum_fusion.1
  202.4 2.8 gather_fusion.4
  205.2 2.6 convert_bitcast_fusion
  207.8 2.7 copy.119
  210.5 2.7 copy.123
  213.2 3.2 multiply_convert_fusion
  219.5 1.8 constant_dynamic-update-slice_fusion.22
  222.4 1.8 constant_dynamic-update-slice_fusion.21
  224.3 6.3 %collective-permute-done.23 = bf16[64,3584]{1,0:T(8,128)(2,1)S(1)} collective-permute-done((bf16[64,3584]{1,0:T(8,128)(2,1)S(1)}, bf16[64,3584]{1,0:T(8,128)(2,1)S(1)}, u32[]{:S(2)}, u32[]{:S(2)}) %collective-permute-start.23) | collective-permute-done | bytes 458784 | tf_op jit(solution)/shard_map/ppermute | solution.py:164
  230.6 2.5 collective-permute-start.17
  235.8 11.4 %collective-permute-done.16 = bf16[64,3584]{1,0:T(8,128)(2,1)S(1)} collective-permute-done((bf16[64,3584]{1,0:T(8,128)(2,1)S(1)}, bf16[64,3584]{1,0:T(8,128)(2,1)S(1)}, u32[]{:S(2)}, u32[]{:S(2)}) %collective-permute-start.16) | collective-permute-done | bytes 458784 | tf_op jit(solution)/shard_map/ppermute | solution.py:164
  250.0 9.4 %collective-permute-done.25 = bf16[64,3584]{1,0:T(8,128)(2,1)S(1)} collective-permute-done((bf16[64,3584]{1,0:T(8,128)(2,1)S(1)}, bf16[64,3584]{1,0:T(8,128)(2,1)S(1)}, u32[]{:S(2)}, u32[]{:S(2)}) %collective-permute-start.25) | collective-permute-done | bytes 458784 | tf_op jit(solution)/shard_map/ppermute | solution.py:164
  261.5 6.4 %collective-permute-done.18 = bf16[64,3584]{1,0:T(8,128)(2,1)S(1)} collective-permute-done((bf16[64,3584]{1,0:T(8,128)(2,1)S(1)}, bf16[64,3584]{1,0:T(8,128)(2,1)S(1)}, u32[]{:S(2)}, u32[]{:S(2)}) %collective-permute-start.18) | collective-permute-done | bytes 458784 | tf_op jit(solution)/shard_map/ppermute | solution.py:164
  270.2 6.2 %collective-permute-done.26 = bf16[64,3584]{1,0:T(8,128)(2,1)S(1)} collective-permute-done((bf16[64,3584]{1,0:T(8,128)(2,1)S(1)}, bf16[64,3584]{1,0:T(8,128)(2,1)S(1)}, u32[]{:S(2)}, u32[]{:S(2)}) %collective-permute-start.26) | collective-permute-done | bytes 458784 | tf_op jit(solution)/shard_map/ppermute | solution.py:164
  280.0 12.2 %collective-permute-done.28 = bf16[64,3584]{1,0:T(8,128)(2,1)S(1)} collective-permute-done((bf16[64,3584]{1,0:T(8,128)(2,1)S(1)}, bf16[64,3584]{1,0:T(8,128)(2,1)S(1)}, u32[]{:S(2)}, u32[]{:S(2)}) %collective-permute-start.28) | collective-permute-done | bytes 458784 | tf_op jit(solution)/shard_map/ppermute | solution.py:164
  293.9 6.7 %collective-permute-done.19 = bf16[64,3584]{1,0:T(8,128)(2,1)S(1)} collective-permute-done((bf16[64,3584]{1,0:T(8,128)(2,1)S(1)}, bf16[64,3584]{1,0:T(8,128)(2,1)S(1)}, u32[]{:S(2)}, u32[]{:S(2)}) %collective-permute-start.19) | collective-permute-done | bytes 458784 | tf_op jit(solution)/shard_map/ppermute | solution.py:164
  305.2 5.7 %collective-permute-done.21 = bf16[64,3584]{1,0:T(8,128)(2,1)S(1)} collective-permute-done((bf16[64,3584]{1,0:T(8,128)(2,1)S(1)}, bf16[64,3584]{1,0:T(8,128)(2,1)S(1)}, u32[]{:S(2)}, u32[]{:S(2)}) %collective-permute-start.21) | collective-permute-done | bytes 458784 | tf_op jit(solution)/shard_map/ppermute | solution.py:164
  313.8 1.8 constant_dynamic-update-slice_fusion.18
  315.7 1.9 constant_dynamic-update-slice_fusion.17
  319.1 9.1 %concatenate.55 = bf16[1024,2048]{0,1:T(8,128)(2,1)} concatenate(bf16[64,2048]{0,1:T(8,128)(2,1)} %bitcast.197, bf16[64,2048]{0,1:T(8,128)(2,1)} %bitcast.199, bf16[64,2048]{0,1:T(8,128)(2,1)} %bitcast.201, bf16[64,2048]{0,1:T(8,128)(2,1)} %bitcast.203, bf16[64,2048]{0,1:T(8,128)(2,1)} %bitcast.195, bf16[64,2048]{0,1:T(8,128)(2,1)} %bitcast.193, bf16[64,2048]{0,1:T(8,128)(2,1)S(1)} %bitcast.191, ...), dimensions={0} | concatenate | bytes 8388608 | tf_op jit(solution)/shard_map/concatenate | solution.py:304
  328.2 20.7 %shard_map.115 = bf16[2048,3584]{1,0:T(8,128)(2,1)} custom-call(s32[16,28]{1,0:T(8,128)S(1)} %copy-done.3, bf16[2048,1024]{1,0:T(8,128)(2,1)} %bitcast.204, bf16[512,3584]{1,0:T(8,128)(2,1)} %constant_dynamic-update-slice_fusion.d0, bf16[512,3584]{1,0:T(8,128)(2,1)} %collective-permute-done.22.d1), custom_call_target="tpu_custom_call" | custom-call | flops 15032385536 | bytes 22020096 | tf_op jit(solution)/shard_map/pallas_call | solution.py:117
  348.8 20.5 %shard_map.116 = bf16[2048,3584]{1,0:T(8,128)(2,1)} custom-call(s32[16,28]{1,0:T(8,128)S(1)} %copy-done.4, bf16[2048,1024]{1,0:T(8,128)(2,1)} %bitcast.205, bf16[512,3584]{1,0:T(8,128)(2,1)} %constant_dynamic-update-slice_fusion.8.d0, bf16[512,3584]{1,0:T(8,128)(2,1)} %collective-permute-done.29.d1), custom_call_target="tpu_custom_call" | custom-call | flops 15032385536 | bytes 22020096 | tf_op jit(solution)/shard_map/pallas_call | solution.py:117
  369.3 20.3 %shard_map.117 = bf16[3584,2048]{1,0:T(8,128)(2,1)} custom-call(s32[28,16]{1,0:T(8,128)S(1)} %copy.115.keep, bf16[512,3584]{1,0:T(8,128)(2,1)} %constant_dynamic-update-slice_fusion.16.m0, bf16[512,3584]{1,0:T(8,128)(2,1)} %collective-permute-done.39.m1, bf16[512,2048]{1,0:T(8,128)(2,1)S(1)} %bitcast_dynamic-update-slice_fusion.2.g0, ...), custom_call_target="tpu_custom_call" | custom-call | flops 15032385536 | bytes 22020096 | tf_op jit(solution)/shard_map/pallas_call | solution.py:146
  (278 shorter events, 106.6 us)
Async XLA Ops:
  18.8 300.2 %collective-permute-start = (bf16[512,2048]{0,1:T(8,128)(2,1)}, bf16[512,2048]{0,1:T(8,128)(2,1)}, u32[]{:S(2)}, u32[]{:S(2)}) collective-permute-start(bf16[512,2048]{0,1:T(8,128)(2,1)} %concatenate.54), channel_id=1, source_target_pairs={{0,16},{16,0},{1,17},{17,1},{2,18},{18,2},{3,19},{19,3},{4,20},{20... | collective-permute-start | bytes 6291464 | tf_op jit(solution)/shard_map/ppermute | solution.py:164
  35.2 50.4 %collective-permute-start.1 = (bf16[2,64,3584]{2,1,0:T(8,128)(2,1)S(1)}, bf16[2,64,3584]{2,1,0:T(8,128)(2,1)}, u32[]{:S(2)}, u32[]{:S(2)}) collective-permute-start(bf16[2,64,3584]{2,1,0:T(8,128)(2,1)S(1)} %dynamic-slice_bitcast_fusion.5), channel_id=1, source_target_pairs={{0,4},{4,0},{8,12},{12,8},{1,5},{5,1},{9,13},{13,9},{2,6},{6,2},{1... | collective-permute-start | bytes 2752520 | tf_op jit(solution)/shard_map/ppermute | solution.py:164
  40.0 51.8 %collective-permute-start.3 = (bf16[2,64,3584]{2,1,0:T(8,128)(2,1)}, bf16[2,64,3584]{2,1,0:T(8,128)(2,1)}, u32[]{:S(2)}, u32[]{:S(2)}) collective-permute-start(bf16[2,64,3584]{2,1,0:T(8,128)(2,1)} %dynamic-slice_bitcast_fusion.4), channel_id=1, source_target_pairs={{0,8},{4,12},{8,0},{12,4},{1,9},{5,13},{9,1},{13,5},{2,10},{6,14},... | collective-permute-start | bytes 2752520 | tf_op jit(solution)/shard_map/ppermute | solution.py:164
  56.9 31.9 %collective-permute-start.12 = (bf16[2,64,3584]{2,1,0:T(8,128)(2,1)}, bf16[2,64,3584]{2,1,0:T(8,128)(2,1)}, u32[]{:S(2)}, u32[]{:S(2)}) collective-permute-start(bf16[2,64,3584]{2,1,0:T(8,128)(2,1)} %dynamic-slice_bitcast_fusion.1), channel_id=1, source_target_pairs={{0,4},{4,0},{8,12},{12,8},{1,5},{5,1},{9,13},{13,9},{2,6},{6,2},{1... | collective-permute-start | bytes 2752520 | tf_op jit(solution)/shard_map/ppermute | solution.py:164
  58.4 37.0 %collective-permute-start.14 = (bf16[2,64,3584]{2,1,0:T(8,128)(2,1)}, bf16[2,64,3584]{2,1,0:T(8,128)(2,1)}, u32[]{:S(2)}, u32[]{:S(2)}) collective-permute-start(bf16[2,64,3584]{2,1,0:T(8,128)(2,1)} %dynamic-slice_bitcast_fusion), channel_id=1, source_target_pairs={{0,8},{4,12},{8,0},{12,4},{1,9},{5,13},{9,1},{13,5},{2,10},{6,14},... | collective-permute-start | bytes 2752520 | tf_op jit(solution)/shard_map/ppermute | solution.py:164
  85.6 23.3 %collective-permute-start.8 = (bf16[2,64,3584]{2,1,0:T(8,128)(2,1)S(1)}, bf16[2,64,3584]{2,1,0:T(8,128)(2,1)S(1)}, u32[]{:S(2)}, u32[]{:S(2)}) collective-permute-start(bf16[2,64,3584]{2,1,0:T(8,128)(2,1)S(1)} %dynamic-slice_bitcast_fusion.3), channel_id=1, source_target_pairs={{0,4},{4,0},{8,12},{12,8},{1,5},{5,1},{9,13},{13,9},{2,6},{6,2},{1... | collective-permute-start | bytes 2752520 | tf_op jit(solution)/shard_map/ppermute | solution.py:164
  88.8 23.8 %collective-permute-start.10 = (bf16[2,64,3584]{2,1,0:T(8,128)(2,1)S(1)}, bf16[2,64,3584]{2,1,0:T(8,128)(2,1)S(1)}, u32[]{:S(2)}, u32[]{:S(2)}) collective-permute-start(bf16[2,64,3584]{2,1,0:T(8,128)(2,1)S(1)} %dynamic-slice_bitcast_fusion.2), channel_id=1, source_target_pairs={{0,8},{4,12},{8,0},{12,4},{1,9},{5,13},{9,1},{13,5},{2,10},{6,14},... | collective-permute-start | bytes 2752520 | tf_op jit(solution)/shard_map/ppermute | solution.py:164
  91.9 30.1 %collective-permute-start.2 = (bf16[64,3584]{1,0:T(8,128)(2,1)S(1)}, bf16[64,3584]{1,0:T(8,128)(2,1)S(1)}, u32[]{:S(2)}, u32[]{:S(2)}) collective-permute-start(bf16[64,3584]{1,0:T(8,128)(2,1)S(1)} %fusion.6), channel_id=1, source_target_pairs={{0,8},{4,12},{8,0},{12,4},{1,9},{5,13},{9,1},{13,5},{2,10},{6,14},... | collective-permute-start | bytes 1376264 | tf_op jit(solution)/shard_map/ppermute | solution.py:164
  94.5 16.1 %copy-start.15 = (bf16[4,1,64,3584]{3,2,1,0:T(8,128)(2,1)S(1)}, bf16[4,1,64,3584]{3,2,1,0:T(8,128)(2,1)}, u32[]{:S(2)}) copy-start(bf16[4,1,64,3584]{3,2,1,0:T(8,128)(2,1)} %get-tuple-element.22) | copy-start | bytes 5505028
  95.4 28.3 %collective-permute-start.4 = (bf16[64,3584]{1,0:T(8,128)(2,1)S(1)}, bf16[64,3584]{1,0:T(8,128)(2,1)S(1)}, u32[]{:S(2)}, u32[]{:S(2)}) collective-permute-start(bf16[64,3584]{1,0:T(8,128)(2,1)S(1)} %fusion.7), channel_id=1, source_target_pairs={{0,4},{4,0},{8,12},{12,8},{1,5},{5,1},{9,13},{13,9},{2,6},{6,2},{1... | collective-permute-start | bytes 1376264 | tf_op jit(solution)/shard_map/ppermute | solution.py:164
  97.3 14.4 %copy-start.17 = (f32[2,64,3584]{2,1,0:T(8,128)}, f32[2,64,3584]{2,1,0:T(8,128)S(1)}, u32[]{:S(2)}) copy-start(f32[2,64,3584]{2,1,0:T(8,128)S(1)} %convert_add_fusion) | copy-start | bytes 5505028
  97.3 16.8 %copy-start.14 = (bf16[4,1,64,3584]{3,2,1,0:T(8,128)(2,1)S(1)}, bf16[4,1,64,3584]{3,2,1,0:T(8,128)(2,1)}, u32[]{:S(2)}) copy-start(bf16[4,1,64,3584]{3,2,1,0:T(8,128)(2,1)} %get-tuple-element.23) | copy-start | bytes 5505028
  108.9 23.0 %collective-permute-start.13 = (bf16[64,3584]{1,0:T(8,128)(2,1)}, bf16[64,3584]{1,0:T(8,128)(2,1)}, u32[]{:S(2)}, u32[]{:S(2)}) collective-permute-start(bf16[64,3584]{1,0:T(8,128)(2,1)} %fusion.10), channel_id=1, source_target_pairs={{0,8},{4,12},{8,0},{12,4},{1,9},{5,13},{9,1},{13,5},{2,10},{6,14},... | collective-permute-start | bytes 1376264 | tf_op jit(solution)/shard_map/ppermute | solution.py:164
  112.6 22.3 %collective-permute-start.15 = (bf16[64,3584]{1,0:T(8,128)(2,1)}, bf16[64,3584]{1,0:T(8,128)(2,1)}, u32[]{:S(2)}, u32[]{:S(2)}) collective-permute-start(bf16[64,3584]{1,0:T(8,128)(2,1)} %fusion.11), channel_id=1, source_target_pairs={{0,4},{4,0},{8,12},{12,8},{1,5},{5,1},{9,13},{13,9},{2,6},{6,2},{1... | collective-permute-start | bytes 1376264 | tf_op jit(solution)/shard_map/ppermute | solution.py:164
  122.0 17.8 %collective-permute-start.9 = (bf16[64,3584]{1,0:T(8,128)(2,1)}, bf16[64,3584]{1,0:T(8,128)(2,1)}, u32[]{:S(2)}, u32[]{:S(2)}) collective-permute-start(bf16[64,3584]{1,0:T(8,128)(2,1)} %fusion.8), channel_id=1, source_target_pairs={{0,8},{4,12},{8,0},{12,4},{1,9},{5,13},{9,1},{13,5},{2,10},{6,14},... | collective-permute-start | bytes 1376264 | tf_op jit(solution)/shard_map/ppermute | solution.py:164
  123.7 17.5 %collective-permute-start.11 = (bf16[64,3584]{1,0:T(8,128)(2,1)}, bf16[64,3584]{1,0:T(8,128)(2,1)}, u32[]{:S(2)}, u32[]{:S(2)}) collective-permute-start(bf16[64,3584]{1,0:T(8,128)(2,1)} %fusion.9), channel_id=1, source_target_pairs={{0,4},{4,0},{8,12},{12,8},{1,5},{5,1},{9,13},{13,9},{2,6},{6,2},{1... | collective-permute-start | bytes 1376264 | tf_op jit(solution)/shard_map/ppermute | solution.py:164
  131.9 62.1 %collective-permute-start.5 = (bf16[7,128,128]{2,1,0:T(8,128)(2,1)}, bf16[7,128,128]{2,1,0:T(8,128)(2,1)}, u32[]{:S(2)}, u32[]{:S(2)}) collective-permute-start(bf16[7,128,128]{2,1,0:T(8,128)(2,1)} %broadcast_select_fusion.6), channel_id=1, source_target_pairs={{0,1},{1,0},{2,3},{3,2},{4,5},{5,4},{6,7},{7,6},{8,9},{9,8},{10,11... | collective-permute-start | bytes 688136 | tf_op jit(solution)/shard_map/ppermute | solution.py:164
  146.2 12.5 %copy-start.41 = (pred[7]{0:T(512)(128)(4,1)S(1)}, pred[7]{0:T(512)(128)(4,1)}, u32[]{:S(2)}) copy-start(pred[7]{0:T(512)(128)(4,1)} %compare_and_fusion.2) | copy-start | bytes 25
  146.2 16.2 %copy-start.39 = (pred[7]{0:T(512)(128)(4,1)S(1)}, pred[7]{0:T(512)(128)(4,1)}, u32[]{:S(2)}) copy-start(pred[7]{0:T(512)(128)(4,1)} %compare_and_fusion.1) | copy-start | bytes 25
  146.2 19.7 %copy-start.40 = (pred[7]{0:T(512)(128)(4,1)S(1)}, pred[7]{0:T(512)(128)(4,1)}, u32[]{:S(2)}) copy-start(pred[7]{0:T(512)(128)(4,1)} %compare_and_fusion.9) | copy-start | bytes 25
  148.7 15.1 %copy-start.42 = (pred[7]{0:T(512)(128)(4,1)S(1)}, pred[7]{0:T(512)(128)(4,1)}, u32[]{:S(2)}) copy-start(pred[7]{0:T(512)(128)(4,1)} %compare_and_fusion.6) | copy-start | bytes 25
  157.1 9.7 %collective-permute-start.30 = (bf16[7,128,128]{2,1,0:T(8,128)(2,1)S(1)}, bf16[7,128,128]{2,1,0:T(8,128)(2,1)S(1)}, u32[]{:S(2)}, u32[]{:S(2)}) collective-permute-start(bf16[7,128,128]{2,1,0:T(8,128)(2,1)S(1)} %broadcast_select_fusion.2), channel_id=1, source_target_pairs={{0,1},{1,0},{2,3},{3,2},{4,5},{5,4},{6,7},{7,6},{8,9},{9,8},{10,11... | collective-permute-start | bytes 688136 | tf_op jit(solution)/shard_map/ppermute | solution.py:164
  159.8 25.6 %collective-permute-start.31 = (bf16[7,128,128]{2,1,0:T(8,128)(2,1)S(1)}, bf16[7,128,128]{2,1,0:T(8,128)(2,1)S(1)}, u32[]{:S(2)}, u32[]{:S(2)}) collective-permute-start(bf16[7,128,128]{2,1,0:T(8,128)(2,1)S(1)} %broadcast_select_fusion.1), channel_id=1, source_target_pairs={{0,2},{1,3},{2,0},{3,1},{4,6},{5,7},{6,4},{7,5},{8,10},{9,11},{10,... | collective-permute-start | bytes 688136 | tf_op jit(solution)/shard_map/ppermute | solution.py:164
  163.4 22.0 %collective-permute-start.32 = (bf16[7,128,128]{2,1,0:T(8,128)(2,1)S(1)}, bf16[7,128,128]{2,1,0:T(8,128)(2,1)S(1)}, u32[]{:S(2)}, u32[]{:S(2)}) collective-permute-start(bf16[7,128,128]{2,1,0:T(8,128)(2,1)S(1)} %broadcast_select_fusion), channel_id=1, source_target_pairs={{0,3},{1,2},{2,1},{3,0},{4,7},{5,6},{6,5},{7,4},{8,11},{9,10},{10,... | collective-permute-start | bytes 688136 | tf_op jit(solution)/shard_map/ppermute | solution.py:164
  166.8 31.0 %collective-permute-start.6 = (bf16[7,128,128]{2,1,0:T(8,128)(2,1)}, bf16[7,128,128]{2,1,0:T(8,128)(2,1)}, u32[]{:S(2)}, u32[]{:S(2)}) collective-permute-start(bf16[7,128,128]{2,1,0:T(8,128)(2,1)} %broadcast_select_fusion.5), channel_id=1, source_target_pairs={{0,2},{1,3},{2,0},{3,1},{4,6},{5,7},{6,4},{7,5},{8,10},{9,11},{10,... | collective-permute-start | bytes 688136 | tf_op jit(solution)/shard_map/ppermute | solution.py:164
  185.3 13.4 %collective-permute-start.7 = (bf16[7,128,128]{2,1,0:T(8,128)(2,1)}, bf16[7,128,128]{2,1,0:T(8,128)(2,1)}, u32[]{:S(2)}, u32[]{:S(2)}) collective-permute-start(bf16[7,128,128]{2,1,0:T(8,128)(2,1)} %broadcast_select_fusion.4), channel_id=1, source_target_pairs={{0,3},{1,2},{2,1},{3,0},{4,7},{5,6},{6,5},{7,4},{8,11},{9,10},{10,... | collective-permute-start | bytes 688136 | tf_op jit(solution)/shard_map/ppermute | solution.py:164
  192.4 28.9 %collective-permute-start.34 = (bf16[64,3584]{1,0:T(8,128)(2,1)}, bf16[64,3584]{1,0:T(8,128)(2,1)}, u32[]{:S(2)}, u32[]{:S(2)}) collective-permute-start(bf16[64,3584]{1,0:T(8,128)(2,1)} %bitcast.169), channel_id=1, source_target_pairs={{0,8},{4,12},{8,0},{12,4},{1,9},{5,13},{9,1},{13,5},{2,10},{6,14},... | collective-permute-start | bytes 1376264 | tf_op jit(solution)/shard_map/ppermute | solution.py:164
  194.0 25.0 %collective-permute-start.33 = (bf16[64,3584]{1,0:T(8,128)(2,1)}, bf16[64,3584]{1,0:T(8,128)(2,1)}, u32[]{:S(2)}, u32[]{:S(2)}) collective-permute-start(bf16[64,3584]{1,0:T(8,128)(2,1)} %bitcast.169), channel_id=1, source_target_pairs={{0,4},{4,0},{8,12},{12,8},{1,5},{5,1},{9,13},{13,9},{2,6},{6,2},{1... | collective-permute-start | bytes 1376264 | tf_op jit(solution)/shard_map/ppermute | solution.py:164
  197.7 117.9 %collective-permute-start.37 = (bf16[64,3584]{1,0:T(8,128)(2,1)}, bf16[64,3584]{1,0:T(8,128)(2,1)}, u32[]{:S(2)}, u32[]{:S(2)}) collective-permute-start(bf16[64,3584]{1,0:T(8,128)(2,1)} %bitcast.168), channel_id=1, source_target_pairs={{0,4},{4,0},{8,12},{12,8},{1,5},{5,1},{9,13},{13,9},{2,6},{6,2},{1... | collective-permute-start | bytes 1376264 | tf_op jit(solution)/shard_map/ppermute | solution.py:164
  198.7 103.7 %collective-permute-start.36 = (bf16[64,3584]{1,0:T(8,128)(2,1)}, bf16[64,3584]{1,0:T(8,128)(2,1)}, u32[]{:S(2)}, u32[]{:S(2)}) collective-permute-start(bf16[64,3584]{1,0:T(8,128)(2,1)} %bitcast.168), channel_id=1, source_target_pairs={{0,8},{4,12},{8,0},{12,4},{1,9},{5,13},{9,1},{13,5},{2,10},{6,14},... | collective-permute-start | bytes 1376264 | tf_op jit(solution)/shard_map/ppermute | solution.py:164
  219.0 14.9 %collective-permute-start.24 = (bf16[64,3584]{1,0:T(8,128)(2,1)S(1)}, bf16[64,3584]{1,0:T(8,128)(2,1)S(1)}, u32[]{:S(2)}, u32[]{:S(2)}) collective-permute-start(bf16[64,3584]{1,0:T(8,128)(2,1)S(1)} %get-tuple-element.42), channel_id=1, source_target_pairs={{0,8},{4,12},{8,0},{12,4},{1,9},{5,13},{9,1},{13,5},{2,10},{6,14},... | collective-permute-start | bytes 1376264 | tf_op jit(solution)/shard_map/ppermute | solution.py:164
  221.4 9.3 %collective-permute-start.23 = (bf16[64,3584]{1,0:T(8,128)(2,1)S(1)}, bf16[64,3584]{1,0:T(8,128)(2,1)S(1)}, u32[]{:S(2)}, u32[]{:S(2)}) collective-permute-start(bf16[64,3584]{1,0:T(8,128)(2,1)S(1)} %get-tuple-element.42), channel_id=1, source_target_pairs={{0,4},{4,0},{8,12},{12,8},{1,5},{5,1},{9,13},{13,9},{2,6},{6,2},{1... | collective-permute-start | bytes 1376264 | tf_op jit(solution)/shard_map/ppermute | solution.py:164
  230.6 18.5 %collective-permute-start.17 = (bf16[64,3584]{1,0:T(8,128)(2,1)S(1)}, bf16[64,3584]{1,0:T(8,128)(2,1)S(1)}, u32[]{:S(2)}, u32[]{:S(2)}) collective-permute-start(bf16[64,3584]{1,0:T(8,128)(2,1)S(1)} %get-tuple-element.45), channel_id=1, source_target_pairs={{0,8},{4,12},{8,0},{12,4},{1,9},{5,13},{9,1},{13,5},{2,10},{6,14},... | collective-permute-start | bytes 1376264 | tf_op jit(solution)/shard_map/ppermute | solution.py:164
  233.9 13.4 %collective-permute-start.16 = (bf16[64,3584]{1,0:T(8,128)(2,1)S(1)}, bf16[64,3584]{1,0:T(8,128)(2,1)S(1)}, u32[]{:S(2)}, u32[]{:S(2)}) collective-permute-start(bf16[64,3584]{1,0:T(8,128)(2,1)S(1)} %get-tuple-element.45), channel_id=1, source_target_pairs={{0,4},{4,0},{8,12},{12,8},{1,5},{5,1},{9,13},{13,9},{2,6},{6,2},{1... | collective-permute-start | bytes 1376264 | tf_op jit(solution)/shard_map/ppermute | solution.py:164
  247.3 30.6 %collective-permute-start.27 = (bf16[64,3584]{1,0:T(8,128)(2,1)S(1)}, bf16[64,3584]{1,0:T(8,128)(2,1)S(1)}, u32[]{:S(2)}, u32[]{:S(2)}) collective-permute-start(bf16[64,3584]{1,0:T(8,128)(2,1)S(1)} %get-tuple-element.40), channel_id=1, source_target_pairs={{0,4},{4,0},{8,12},{12,8},{1,5},{5,1},{9,13},{13,9},{2,6},{6,2},{1... | collective-permute-start | bytes 1376264 | tf_op jit(solution)/shard_map/ppermute | solution.py:164
  249.2 10.2 %collective-permute-start.25 = (bf16[64,3584]{1,0:T(8,128)(2,1)S(1)}, bf16[64,3584]{1,0:T(8,128)(2,1)S(1)}, u32[]{:S(2)}, u32[]{:S(2)}) collective-permute-start(bf16[64,3584]{1,0:T(8,128)(2,1)S(1)} %collective-permute-done.23), channel_id=1, source_target_pairs={{0,8},{4,12},{8,0},{12,4},{1,9},{5,13},{9,1},{13,5},{2,10},{6,14},... | collective-permute-start | bytes 1376264 | tf_op jit(solution)/shard_map/ppermute | solution.py:164
  259.4 8.5 %collective-permute-start.18 = (bf16[64,3584]{1,0:T(8,128)(2,1)S(1)}, bf16[64,3584]{1,0:T(8,128)(2,1)S(1)}, u32[]{:S(2)}, u32[]{:S(2)}) collective-permute-start(bf16[64,3584]{1,0:T(8,128)(2,1)S(1)} %collective-permute-done.16), channel_id=1, source_target_pairs={{0,8},{4,12},{8,0},{12,4},{1,9},{5,13},{9,1},{13,5},{2,10},{6,14},... | collective-permute-start | bytes 1376264 | tf_op jit(solution)/shard_map/ppermute | solution.py:164
  267.9 8.5 %collective-permute-start.26 = (bf16[64,3584]{1,0:T(8,128)(2,1)S(1)}, bf16[64,3584]{1,0:T(8,128)(2,1)S(1)}, u32[]{:S(2)}, u32[]{:S(2)}) collective-permute-start(bf16[64,3584]{1,0:T(8,128)(2,1)S(1)} %get-tuple-element.40), channel_id=1, source_target_pairs={{0,8},{4,12},{8,0},{12,4},{1,9},{5,13},{9,1},{13,5},{2,10},{6,14},... | collective-permute-start | bytes 1376264 | tf_op jit(solution)/shard_map/ppermute | solution.py:164
  276.3 27.2 %collective-permute-start.20 = (bf16[64,3584]{1,0:T(8,128)(2,1)S(1)}, bf16[64,3584]{1,0:T(8,128)(2,1)S(1)}, u32[]{:S(2)}, u32[]{:S(2)}) collective-permute-start(bf16[64,3584]{1,0:T(8,128)(2,1)S(1)} %get-tuple-element.43), channel_id=1, source_target_pairs={{0,4},{4,0},{8,12},{12,8},{1,5},{5,1},{9,13},{13,9},{2,6},{6,2},{1... | collective-permute-start | bytes 1376264 | tf_op jit(solution)/shard_map/ppermute | solution.py:164
  277.9 14.3 %collective-permute-start.28 = (bf16[64,3584]{1,0:T(8,128)(2,1)S(1)}, bf16[64,3584]{1,0:T(8,128)(2,1)S(1)}, u32[]{:S(2)}, u32[]{:S(2)}) collective-permute-start(bf16[64,3584]{1,0:T(8,128)(2,1)S(1)} %collective-permute-done.26), channel_id=1, source_target_pairs={{0,4},{4,0},{8,12},{12,8},{1,5},{5,1},{9,13},{13,9},{2,6},{6,2},{1... | collective-permute-start | bytes 1376264 | tf_op jit(solution)/shard_map/ppermute | solution.py:164
  292.2 8.5 %collective-permute-start.19 = (bf16[64,3584]{1,0:T(8,128)(2,1)S(1)}, bf16[64,3584]{1,0:T(8,128)(2,1)S(1)}, u32[]{:S(2)}, u32[]{:S(2)}) collective-permute-start(bf16[64,3584]{1,0:T(8,128)(2,1)S(1)} %get-tuple-element.43), channel_id=1, source_target_pairs={{0,8},{4,12},{8,0},{12,4},{1,9},{5,13},{9,1},{13,5},{2,10},{6,14},... | collective-permute-start | bytes 1376264 | tf_op jit(solution)/shard_map/ppermute | solution.py:164
  300.7 11.0 %collective-permute-start.35 = (bf16[64,3584]{1,0:T(8,128)(2,1)}, bf16[64,3584]{1,0:T(8,128)(2,1)S(1)}, u32[]{:S(2)}, u32[]{:S(2)}) collective-permute-start(bf16[64,3584]{1,0:T(8,128)(2,1)} %collective-permute-done.33), channel_id=1, source_target_pairs={{0,8},{4,12},{8,0},{12,4},{1,9},{5,13},{9,1},{13,5},{2,10},{6,14},... | collective-permute-start | bytes 1376264 | tf_op jit(solution)/shard_map/ppermute | solution.py:164
  302.4 8.5 %collective-permute-start.21 = (bf16[64,3584]{1,0:T(8,128)(2,1)S(1)}, bf16[64,3584]{1,0:T(8,128)(2,1)S(1)}, u32[]{:S(2)}, u32[]{:S(2)}) collective-permute-start(bf16[64,3584]{1,0:T(8,128)(2,1)S(1)} %collective-permute-done.19), channel_id=1, source_target_pairs={{0,4},{4,0},{8,12},{12,8},{1,5},{5,1},{9,13},{13,9},{2,6},{6,2},{1... | collective-permute-start | bytes 1376264 | tf_op jit(solution)/shard_map/ppermute | solution.py:164
  303.5 14.0 %collective-permute-start.38 = (bf16[64,3584]{1,0:T(8,128)(2,1)}, bf16[64,3584]{1,0:T(8,128)(2,1)S(1)}, u32[]{:S(2)}, u32[]{:S(2)}) collective-permute-start(bf16[64,3584]{1,0:T(8,128)(2,1)} %collective-permute-done.36), channel_id=1, source_target_pairs={{0,4},{4,0},{8,12},{12,8},{1,5},{5,1},{9,13},{13,9},{2,6},{6,2},{1... | collective-permute-start | bytes 1376264 | tf_op jit(solution)/shard_map/ppermute | solution.py:164
  310.9 38.0 %collective-permute-start.29 = (bf16[512,3584]{1,0:T(8,128)(2,1)}, bf16[512,3584]{1,0:T(8,128)(2,1)}, u32[]{:S(2)}, u32[]{:S(2)}) collective-permute-start(bf16[512,3584]{1,0:T(8,128)(2,1)} %constant_dynamic-update-slice_fusion.8.d0), channel_id=1, source_target_pairs={{0,16},{16,0},{1,17},{17,1},{2,18},{18,2},{3,19},{19,3},{4,20},{20... | collective-permute-start | bytes 11010056 | tf_op jit(solution)/shard_map/ppermute | solution.py:164
  311.7 16.5 %collective-permute-start.22 = (bf16[512,3584]{1,0:T(8,128)(2,1)}, bf16[512,3584]{1,0:T(8,128)(2,1)}, u32[]{:S(2)}, u32[]{:S(2)}) collective-permute-start(bf16[512,3584]{1,0:T(8,128)(2,1)} %constant_dynamic-update-slice_fusion.d0), channel_id=1, source_target_pairs={{0,16},{16,0},{1,17},{17,1},{2,18},{18,2},{3,19},{19,3},{4,20},{20... | collective-permute-start | bytes 11010056 | tf_op jit(solution)/shard_map/ppermute | solution.py:164
  318.4 51.0 %collective-permute-start.39 = (bf16[512,3584]{1,0:T(8,128)(2,1)}, bf16[512,3584]{1,0:T(8,128)(2,1)}, u32[]{:S(2)}, u32[]{:S(2)}) collective-permute-start(bf16[512,3584]{1,0:T(8,128)(2,1)} %constant_dynamic-update-slice_fusion.16.m0), channel_id=1, source_target_pairs={{0,16},{16,0},{1,17},{17,1},{2,18},{18,2},{3,19},{19,3},{4,20},{20... | collective-permute-start | bytes 11010056 | tf_op jit(solution)/shard_map/ppermute | solution.py:164
  318.5 50.8 %collective-permute-start.40 = (bf16[512,2048]{1,0:T(8,128)(2,1)S(1)}, bf16[512,2048]{1,0:T(8,128)(2,1)}, u32[]{:S(2)}, u32[]{:S(2)}) collective-permute-start(bf16[512,2048]{1,0:T(8,128)(2,1)S(1)} %bitcast_dynamic-update-slice_fusion.2.g0), channel_id=1, source_target_pairs={{0,16},{16,0},{1,17},{17,1},{2,18},{18,2},{3,19},{19,3},{4,20},{20... | collective-permute-start | bytes 6291464 | tf_op jit(solution)/shard_map/ppermute | solution.py:164
  (36 other events, 179.8 us)

commit v2 on v1

--- a/solution.py
+++ b/solution.py
@@ -99,13 +99,15 @@
             ).astype(BF16)
 
 
-def in_grad_kernel(tb, strip, keep, xt, d0, d1, out):
+def in_grad_kernel(tb, strip, keep, xt, d0, d1, out, both):
     col0 = pl.program_id(0) * tb
     half = d0.shape[0]
+    both[:half] = d0[...]
+    both[half:] = d1[...]
     for base in range(0, xt.shape[0], strip):
         value = lax.dot_general(
-            xt[base : base + strip, :half], d0[...], NN, preferred_element_type=F32
-        ) + lax.dot_general(xt[base : base + strip, half:], d1[...], NN, preferred_element_type=F32)
+            xt[base : base + strip], both[...], NN, preferred_element_type=F32
+        )
         store_masked(out, value, keep, base // BLK, col0, base)
 
 
@@ -125,22 +127,24 @@
             pl.BlockSpec((half, tn), lambda j: (0, j)),
         ],
         out_specs=pl.BlockSpec((rows, tn), lambda j: (0, j)),
+        scratch_shapes=[pltpu.VMEM((2 * half, tn), BF16)],
         compiler_params=params(),
         cost_estimate=cost(rows, depth, cols, 2 * depth * cols + 2 * rows * cols),
     )(keep, xt, d0, d1)
 
 
-def out_grad_kernel(tb, keep, m0, m1, g0, g1, out):
+def out_grad_kernel(tb, keep, m0, m1, grads, out, both):
     row0 = pl.program_id(0) * tb
-    value = lax.dot_general(m0[...], g0[...], TN, preferred_element_type=F32) + lax.dot_general(
-        m1[...], g1[...], TN, preferred_element_type=F32
-    )
+    half = m0.shape[0]
+    both[:half] = m0[...]
+    both[half:] = m1[...]
+    value = lax.dot_general(both[...], grads[...], TN, preferred_element_type=F32)
     store_masked(out, value, keep, row0, 0, 0)
 
 
-def down_grad(m0, m1, g0, g1, keep):
+def down_grad(m0, m1, grads, keep):
     half, rows = m0.shape
-    cols = g0.shape[1]
+    cols = grads.shape[1]
     tb = tile_blocks(rows // BLK)
     tm = tb * BLK
     return pl.pallas_call(
@@ -151,13 +155,54 @@
             pl.BlockSpec(memory_space=pltpu.SMEM),
             pl.BlockSpec((half, tm), lambda j: (0, j)),
             pl.BlockSpec((half, tm), lambda j: (0, j)),
-            pl.BlockSpec((half, cols), lambda j: (0, 0)),
-            pl.BlockSpec((half, cols), lambda j: (0, 0)),
+            pl.BlockSpec((2 * half, cols), lambda j: (0, 0)),
         ],
         out_specs=pl.BlockSpec((tm, cols), lambda j: (j, 0)),
+        scratch_shapes=[pltpu.VMEM((2 * half, tm), BF16)],
         compiler_params=params(),
         cost_estimate=cost(rows, 2 * half, cols, 4 * half * rows + 2 * rows * cols),
-    )(keep, m0, m1, g0, g1)
+    )(keep, m0, m1, grads)
+
+
+def pick_kernel(idx, x, out):
+    for k in range(out.shape[0]):
+        out[k] = x[:, pl.ds(pl.multiple_of(idx[k] * BLK, BLK), BLK)]
+
+
+def pick(x, idx):
+    return pl.pallas_call(
+        pick_kernel,
+        out_shape=jax.ShapeDtypeStruct((idx.shape[0], x.shape[0], BLK), x.dtype),
+        in_specs=[
+            pl.BlockSpec(memory_space=pltpu.SMEM),
+            pl.BlockSpec(memory_space=pltpu.VMEM),
+        ],
+        out_specs=pl.BlockSpec(memory_space=pltpu.VMEM),
+        compiler_params=params(),
+        cost_estimate=cost(1, 1, 1, 4 * x.size),
+    )(idx, x)
+
+
+def place_kernel(cap, idx, *refs):
+    *parts, out, held = refs
+    for p, part in enumerate(parts):
+        held[p * cap : (p + 1) * cap] = part[...]
+    for k in range(out.shape[1] // BLK):
+        out[:, k * BLK : (k + 1) * BLK] = held[idx[k]]
+
+
+def place(parts, idx):
+    cap, rows, _ = parts[0].shape
+    return pl.pallas_call(
+        functools.partial(place_kernel, cap),
+        out_shape=jax.ShapeDtypeStruct((rows, idx.shape[0] * BLK), BF16),
+        in_specs=[pl.BlockSpec(memory_space=pltpu.SMEM)]
+        + [pl.BlockSpec(memory_space=pltpu.VMEM)] * len(parts),
+        out_specs=pl.BlockSpec(memory_space=pltpu.VMEM),
+        scratch_shapes=[pltpu.VMEM((cap * len(parts), rows, BLK), BF16)],
+        compiler_params=params(),
+        cost_estimate=cost(1, 1, 1, 4 * rows * idx.shape[0] * BLK),
+    )(idx, *parts)
 
 
 def swap(x, axis, n, bits):
@@ -173,17 +218,28 @@
     rows, cols = part.shape
     levels = n.bit_length() - 1
     piece = rows // (2 * n)
-    split = part.reshape(n, 2, piece, cols)
+    dests = (2,) * levels
+    split = part.reshape(dests + (2, piece, cols))
     halves = []
     for half, order in enumerate(mp_orders(n)):
-        cur = split[:, half].reshape((2,) * levels + (piece, cols))
+        cur = None
         left = list(range(levels))[::-1]
         for stride in order:
-            bit = stride.bit_length() - 1
-            axis = left.index(bit)
+            axis = left.index(stride.bit_length() - 1)
             mine = (me // stride) % 2
-            sent = lax.dynamic_index_in_dim(cur, 1 - mine, axis, keepdims=False)
-            kept = lax.dynamic_index_in_dim(cur, mine, axis, keepdims=False)
+            if cur is None:
+                start = [0] * (levels + 3)
+                start[levels] = half
+                size = list(dests) + [1, piece, cols]
+                size[axis] = 1
+                shape = (2,) * (levels - 1) + (piece, cols)
+                start[axis] = 1 - mine
+                sent = lax.dynamic_slice(split, start, size).reshape(shape)
+                start[axis] = mine
+                kept = lax.dynamic_slice(split, start, size).reshape(shape)
+            else:
+                sent = lax.dynamic_index_in_dim(cur, 1 - mine, axis, keepdims=False)
+                kept = lax.dynamic_index_in_dim(cur, mine, axis, keepdims=False)
             got = swap(sent.astype(BF16), "mp", n, stride)
             cur = kept.astype(F32) + got.astype(F32)
             left.pop(axis)
@@ -191,44 +247,29 @@
     return jnp.concatenate(halves, 0)
 
 
-def gather_tokens(own, n):
+def gather_pieces(own, n, first=None):
+    if n != 4:
+        return [own] + [swap(own, "mp", n, s) for s in range(1, n)]
     piece = own.shape[0] // 2
-    out = []
-    for half, order in enumerate(mp_orders(n)):
-        pieces = [own[half * piece : (half + 1) * piece]]
-        for stride in order:
-            pieces += [swap(p, "mp", n, stride) for p in pieces]
-        out += pieces
-    return jnp.concatenate(out, 0)
+    one = swap(own, "mp", n, 1)
+    two = swap(own, "mp", n, 2)
+    if first is not None:
+        one, two = after(first, (one, two))
+    return [own, one, two, swap(one[:piece], "mp", n, 2), swap(two[piece:], "mp", n, 1)]
 
 
 def gathered_order(x, n, me):
-    piece = x.shape[0] // (2 * n)
-    split = x.reshape(n, 2, piece, x.shape[1])
-    out = []
-    for half, order in enumerate(mp_orders(n)):
-        offsets = [0]
-        for stride in order:
-            offsets += [o ^ stride for o in offsets]
-        for o in offsets:
-            out.append(lax.dynamic_index_in_dim(split[:, half], me ^ o, 0, keepdims=False))
-    return jnp.concatenate(out, 0)
-
-
-def to_blocks(x):
-    return x.reshape(x.shape[0], -1, BLK).transpose(1, 0, 2)
-
-
-def from_blocks(x):
-    return x.transpose(1, 0, 2).reshape(x.shape[1], -1)
-
-
-def exchange(blocks, picks, back, n, me):
-    parts = []
-    for s in range(n):
-        part = jnp.take(blocks, lax.dynamic_index_in_dim(picks, me ^ s, 0, keepdims=False), axis=0)
-        parts.append(part if s == 0 else swap(part, "hidden", n, s))
-    return jnp.take(jnp.concatenate(parts, 0), back, axis=0)
+    split = x.reshape(n, x.shape[0] // n, x.shape[1])
+    return jnp.concatenate(
+        [lax.dynamic_index_in_dim(split, me ^ s, 0, keepdims=False) for s in range(n)], 0
+    )
+
+
+def exchange(x, picks, n):
+    cap = picks.shape[0] // n
+    blocks = pick(x, picks)
+    parts = [blocks[s * cap : (s + 1) * cap] for s in range(n)]
+    return [parts[0]] + [swap(parts[s], "hidden", n, s) for s in range(1, n)]
 
 
 def tables(hidden_order, n, me):
@@ -243,73 +284,64 @@
     slots = jnp.arange(cap, dtype=jnp.int32)
     my_src = lax.dynamic_index_in_dim(src, me, 0, keepdims=False)
     my_rank = lax.dynamic_index_in_dim(rank, me, 0, keepdims=False)
+    stored_back = (my_src ^ me) * cap + my_rank
+    places = jnp.arange(n * cap, dtype=jnp.int32)
     stored_pick = jnp.sum(
-        jnp.where(
-            (my_src[None, None, :] == devs[:, None, None])
-            & (my_rank[None, None, :] == slots[None, :, None]),
-            k[None, None, :],
-            0,
-        ),
-        axis=2,
-    )
-    hidden_pick = jnp.sum(
-        jnp.where(
-            (src[:, None, :] == me) & (rank[:, None, :] == slots[None, :, None]),
-            (ids - me * per)[:, None, :],
-            0,
-        ),
-        axis=2,
-    )
-    stored_back = (my_src ^ me) * cap + my_rank
+        jnp.where(stored_back[None, :] == places[:, None], k[None, :], 0), axis=1
+    )
+    at = (devs ^ me)[:, None] * cap + rank
     wanted = me * per + k
     hidden_back = jnp.sum(
-        jnp.where(
-            ids[None] == wanted[:, None, None],
-            ((devs ^ me)[:, None] * cap + rank)[None],
-            0,
-        ),
+        jnp.where(ids[None] == wanted[:, None, None], at[None], 0), axis=(1, 2)
+    )
+    hidden_pick = jnp.sum(
+        jnp.where((src == me)[None] & (at[None] == places[:, None, None]), (ids - me * per)[None], 0),
         axis=(1, 2),
     )
     return stored_pick, stored_back, hidden_pick, hidden_back
+
+
+def after(first, value):
+    return lax.optimization_barrier((value, first))[0]
 
 
 def shards(n_dp, n_mp, n_hidden, tokens, out_grad, gate_weight, up_weight, down_weight, gate_keep, up_keep, down_keep, hidden_order):
     mp = lax.axis_index("mp")
     here = lax.axis_index("hidden")
-    stored_pick, stored_back, hidden_pick, hidden_back = tables(hidden_order, n_hidden, here)
-
-    grad_part = times_rows(out_grad, down_weight, down_keep)
+
     gate_part = times_columns(tokens, gate_weight, gate_keep)
-    up_part = times_columns(tokens, up_weight, up_keep)
-
-    grad_stored = scatter_sum(grad_part, n_mp, mp).astype(BF16)
-    hidden_grad = from_blocks(
-        exchange(to_blocks(grad_stored), stored_pick, hidden_back, n_hidden, here)
-    )
+    up_part = times_columns(tokens, up_weight, after(gate_part, up_keep))
+    grad_part = times_rows(out_grad, down_weight, after(up_part, down_keep))
+    order = after(gate_part, hidden_order)
+    stored_pick, stored_back, hidden_pick, hidden_back = tables(order, n_hidden, here)
+
     gate = scatter_sum(gate_part, n_mp, mp)
     up = scatter_sum(up_part, n_mp, mp)
-
     sig = jax.nn.sigmoid(gate)
     act = gate * sig
     hidden_act = (act * up).astype(BF16)
-    moved = from_blocks(
-        exchange(to_blocks(hidden_act), hidden_pick, stored_back, n_hidden, here)
-    )
-    hidden_grad = hidden_grad.astype(F32)
+    moved = place(exchange(hidden_act, hidden_pick, n_hidden), stored_back)
+
+    grad_stored = scatter_sum(grad_part, n_mp, mp).astype(BF16)
+    arrived = exchange(grad_stored, stored_pick, n_hidden)
+    hidden_grad = place(arrived, after(moved, hidden_back)).astype(F32)
     gate_delta = (hidden_grad * up * (sig * (1.0 + gate * (1.0 - sig)))).astype(BF16)
     up_delta = (hidden_grad * act).astype(BF16)
 
-    tok = gathered_order(tokens, n_mp, mp)
-    grd = gathered_order(out_grad, n_mp, mp)
+    late_tokens, late_grads = after(grad_part, (tokens, out_grad))
+    tok = gathered_order(late_tokens, n_mp, mp)
+    grd = gathered_order(late_grads, n_mp, mp)
+    grd = jnp.concatenate([grd, swap(grd, "dp", n_dp, 1)], 0)
     tok_t = jnp.concatenate([tok, swap(tok, "dp", n_dp, 1)], 0).T
-    grd_other = swap(grd, "dp", n_dp, 1)
-
-    gate_all = gather_tokens(gate_delta, n_mp)
-    gate_grad = in_grad(tok_t, gate_all, swap(gate_all, "dp", n_dp, 1), gate_keep)
-    up_all = gather_tokens(up_delta, n_mp)
-    up_grad = in_grad(tok_t, up_all, swap(up_all, "dp", n_dp, 1), up_keep)
-    moved_all = gather_tokens(moved, n_mp)
-    down = down_grad(moved_all, swap(moved_all, "dp", n_dp, 1), grd, grd_other, down_keep)
+
+    moved_all = jnp.concatenate(gather_pieces(moved, n_mp), 0)
+    down = down_grad(moved_all, swap(moved_all, "dp", n_dp, 1), grd, down_keep)
+    gate_all = jnp.concatenate(gather_pieces(gate_delta, n_mp), 0)
+    gate_other = after(down, swap(gate_all, "dp", n_dp, 1))
+    gate_grad = in_grad(tok_t, gate_all, gate_other, gate_keep)
+    up_all = jnp.concatenate(gather_pieces(up_delta, n_mp, down), 0)
+    up_other = after(gate_grad, swap(up_all, "dp", n_dp, 1))
+    up_grad = in_grad(tok_t, up_all, up_other, up_keep)
     return gate_grad, up_grad, down
 
 

time: 392 us -> 314 us (0.80)
  local copies, waits for them, and re-layouts: 102 us -> 37.3 us
  other arithmetic: 37.7 us -> 15.2 us
  waiting for transfers between devices: 108 us -> 120 us
  starting transfers between devices: 42.3 us -> 36.9 us
    gather x10 -> x0, local copies, waits for them, and re-layouts: 19.1 us -> none  [the longest x8 13.5 us: exchange(): jnp.take(blocks, lax.dynamic_index_in_dim(picks, me ^ s, 0, keepdims=Fals...]
    unnamed x123 -> x67, local copies, waits for them, and re-layouts: 34.3 us -> 20.6 us
    ppermute x41 -> x35, waiting for transfers between devices: 108 us -> 120 us  [swap(): return lax.ppermute(x, axis, [(i, i ^ bits) for i in range(n)])]
    slice x9 -> x8, local copies, waits for them, and re-layouts: 10.7 us -> 2.39 us  [the longest x3 1.11 us: gather_pieces(): one[:piece]]
    squeeze x6 -> x0, local copies, waits for them, and re-layouts: 8.23 us -> none  [scatter_sum(): sent = lax.dynamic_index_in_dim(cur, 1 - mine, axis, keepdims=False)]
    select_n x17 -> x0, other arithmetic: 8.03 us -> none  [the longest x16 8.03 us: exchange(): jnp.take(blocks, lax.dynamic_index_in_dim(picks, me ^ s, 0, keepdims=Fals...]
    reshape x1 -> x6, local copies, waits for them, and re-layouts: 0.08 us -> 7.56 us  [scatter_sum(): sent = lax.dynamic_slice(split, start, size).reshape(shape)]
    concatenate x1, local copies, waits for them, and re-layouts: 9.08 us -> 1.91 us  [shards(): tok_t = jnp.concatenate([tok, swap(tok, 'dp', n_dp, 1)], 0).T]
  transfers between devices with their start and end apart: 41 -> 35, of which waited for: 14 -> 16; matrix products, arithmetic and copies ran while one was open for 30% -> 14% of each run, Pallas kernels for 20% -> 22%
where the time goes in v2:
time: 314 us; the launch traced here: 313 us
  waiting for transfers between devices  120 us (38%)
  Pallas kernels  102 us (32%)
  local copies, waits for them, and re-layouts  37.3 us (12%)
  starting transfers between devices  36.9 us (12%)
  other arithmetic  15.2 us (5%)
    ppermute x35, waiting for transfers between devices, swap(): return lax.ppermute(x, axis, [(i, i ^ bits) for i in range(n)])  120 us
    pallas_call x2, Pallas kernels, in_grad(): pl.pallas_call(functools.partial(in_grad_kernel, tb, min(512, rows)), gri...  41 us
    ppermute x35, starting transfers between devices, swap(): return lax.ppermute(x, axis, [(i, i ^ bits) for i in range(n)])  36.9 us
    pallas_call x2, Pallas kernels, times_columns(): pl.pallas_call(functools.partial(columns_kernel, tb), grid=(cols // tn,),...  24.7 us
    pallas_call x1, Pallas kernels, down_grad(): pl.pallas_call(functools.partial(out_grad_kernel, tb), grid=(rows // tm,)...  21 us
    unnamed x67, local copies, waits for them, and re-layouts  20.6 us
    pallas_call x1, Pallas kernels, times_rows(): pl.pallas_call(functools.partial(rows_kernel, tb), grid=(cols // tn,), ou...  12.7 us
    reshape x6, local copies, waits for them, and re-layouts, scatter_sum(): sent = lax.dynamic_slice(split, start, size).reshape(shape)  7.56 us
  transfers between devices with their start and end apart: 35, of which 16 were waited for; matrix products, arithmetic and copies ran while one was open for 14% of the time, Pallas kernels for 22%

profile of v2, /device:TPU:0, one launch (start us, length us, event | category | flops | bytes accessed | tf_op | source)
XLA Modules:
  0.0 312.9 jit_solution(16005877289807526879)
XLA Ops:
  0.7 1.6 copy-done.7
  2.9 12.3 %shard_map.112 = bf16[512,3584]{1,0:T(8,128)(2,1)S(1)} custom-call(s32[16,28]{1,0:T(8,128)S(1)} %copy-done.12, bf16[512,2048]{1,0:T(8,128)(2,1)S(1)} %copy-done.7, bf16[2048,3584]{1,0:T(8,128)(2,1)} %w.3), custom_call_target="tpu_custom_call" | custom-call | flops 7516192768 | bytes 18350080 | tf_op jit(solution)/shard_map/pallas_call | solution.py:55
  15.3 1.8 copy-done
  18.2 2.9 collective-permute-start.1
  21.1 2.2 dynamic-slice_bitcast_fusion.4
  23.3 1.5 collective-permute-start.3
  24.8 12.3 %shard_map.113 = bf16[512,3584]{1,0:T(8,128)(2,1)S(1)} custom-call(s32[16,28]{1,0:T(8,128)S(1)} %copy-done.14, bf16[512,2048]{1,0:T(8,128)(2,1)S(1)} %copy-done.8, bf16[2048,3584]{1,0:T(8,128)(2,1)} %w.4), custom_call_target="tpu_custom_call" | custom-call | flops 7516192768 | bytes 18350080 | tf_op jit(solution)/shard_map/pallas_call | solution.py:55
  41.1 12.7 %shard_map.114 = bf16[512,3584]{1,0:T(8,128)(2,1)S(1)} custom-call(s32[28,16]{1,0:T(8,128)S(1)} %copy.66.keep, bf16[512,2048]{1,0:T(8,128)(2,1)S(1)} %copy-done.6, bf16[3584,2048]{1,0:T(8,128)(2,1)} %w.5), custom_call_target="tpu_custom_call" | custom-call | flops 7516192768 | bytes 18350080 | tf_op jit(solution)/shard_map/pallas_call | solution.py:76
  53.8 1.8 copy-done.2
  63.6 1.6 collective-permute-start.14
  65.2 1.8 convert_add_fusion.5
  67.1 1.3 collective-permute-start.4
  69.4 2.2 convert_add_fusion.3
  72.5 9.4 %collective-permute-done.12 = bf16[2,64,3584]{2,1,0:T(8,128)(2,1)} collective-permute-done((bf16[2,64,3584]{2,1,0:T(8,128)(2,1)}, bf16[2,64,3584]{2,1,0:T(8,128)(2,1)}, u32[]{:S(2)}, u32[]{:S(2)}) %collective-permute-start.12) | collective-permute-done | bytes 917536 | tf_op jit(solution)/shard_map/ppermute | solution.py:209
  81.9 2.1 collective-permute-start.6
  84.0 3.0 collective-permute-done.14
  87.0 1.6 convert_add_fusion.1
  90.0 1.6 collective-permute-done.4
  91.7 2.1 collective-permute-start.13
  93.8 3.0 collective-permute-done.2
  96.9 4.6 %collective-permute-done.8 = bf16[64,3584]{1,0:T(8,128)(2,1)S(1)} collective-permute-done((bf16[64,3584]{1,0:T(8,128)(2,1)S(1)}, bf16[64,3584]{1,0:T(8,128)(2,1)S(1)}, u32[]{:S(2)}, u32[]{:S(2)}) %collective-permute-start.8) | collective-permute-done | bytes 458784 | tf_op jit(solution)/shard_map/ppermute | solution.py:209
  101.6 5.1 %collective-permute-done.6 = bf16[64,3584]{1,0:T(8,128)(2,1)S(1)} collective-permute-done((bf16[64,3584]{1,0:T(8,128)(2,1)S(1)}, bf16[64,3584]{1,0:T(8,128)(2,1)S(1)}, u32[]{:S(2)}, u32[]{:S(2)}) %collective-permute-start.6) | collective-permute-done | bytes 458784 | tf_op jit(solution)/shard_map/ppermute | solution.py:209
  108.1 3.7 %collective-permute-start.11 = (bf16[7,128,128]{2,1,0:T(8,128)(2,1)S(1)}, bf16[7,128,128]{2,1,0:T(8,128)(2,1)S(1)}, u32[]{:S(2)}, u32[]{:S(2)}) collective-permute-start(bf16[7,128,128]{2,1,0:T(8,128)(2,1)S(1)} %get-tuple-element.55), channel_id=1, source_target_pairs={{0,3},{1,2},{2,1},{3,0},{4,7},{5,6},{6,5},{7,4},{8,11},{9,10},{10,... | collective-permute-start | bytes 688136 | tf_op jit(solution)/shard_map/ppermute | solution.py:209
  112.7 1.6 collective-permute-done.13
  118.0 8.8 %collective-permute-done.10.refs_2_ = bf16[7,128,128]{2,1,0:T(8,128)(2,1)S(1)} collective-permute-done((bf16[7,128,128]{2,1,0:T(8,128)(2,1)S(1)}, bf16[7,128,128]{2,1,0:T(8,128)(2,1)S(1)}, u32[]{:S(2)}, u32[]{:S(2)}) %collective-permute-start.10) | collective-permute-done | bytes 229408 | tf_op jit(solution)/shard_map/ppermute | solution.py:209
  127.6 1.6 collective-permute-start.25
  129.2 1.4 collective-permute-start.24
  130.6 2.6 collective-permute-start.18
  133.2 1.9 collective-permute-start.16
  135.1 1.6 pad_maximum_fusion.1
  136.7 4.4 %collective-permute-done.18.refs_3_ = bf16[7,128,128]{2,1,0:T(8,128)(2,1)S(1)} collective-permute-done((bf16[7,128,128]{2,1,0:T(8,128)(2,1)S(1)}, bf16[7,128,128]{2,1,0:T(8,128)(2,1)S(1)}, u32[]{:S(2)}, u32[]{:S(2)}) %collective-permute-start.18) | collective-permute-done | bytes 229408 | tf_op jit(solution)/shard_map/ppermute | solution.py:209
  141.1 9.5 %collective-permute-done.17.refs_2_ = bf16[7,128,128]{2,1,0:T(8,128)(2,1)S(1)} collective-permute-done((bf16[7,128,128]{2,1,0:T(8,128)(2,1)S(1)}, bf16[7,128,128]{2,1,0:T(8,128)(2,1)S(1)}, u32[]{:S(2)}, u32[]{:S(2)}) %collective-permute-start.17) | collective-permute-done | bytes 229408 | tf_op jit(solution)/shard_map/ppermute | solution.py:209
  155.8 7.7 %collective-permute-done.26 = bf16[64,3584]{1,0:T(8,128)(2,1)S(1)} collective-permute-done((bf16[64,3584]{1,0:T(8,128)(2,1)S(1)}, bf16[64,3584]{1,0:T(8,128)(2,1)S(1)}, u32[]{:S(2)}, u32[]{:S(2)}) %collective-permute-start.26) | collective-permute-done | bytes 458784 | tf_op jit(solution)/shard_map/ppermute | solution.py:209
  165.0 2.3 constant_dynamic-update-slice_fusion.24
  167.4 1.4 collective-permute-start.19
  170.5 1.6 pad_maximum_fusion
  172.2 1.6 collective-permute-start.31
  173.8 3.2 %constant_dynamic-update-slice_fusion.15.grads = bf16[1024,2048]{1,0:T(8,128)(2,1)} fusion(bf16[1024,2048]{1,0:T(8,128)(2,1)} %get-tuple-element.27, bf16[512,2048]{1,0:T(8,128)(2,1)} %collective-permute-done.29), kind=kLoop, calls=%fused_computation.69 | loop fusion | bytes 4194304 | tf_op jit(solution)/shard_map/concatenate | solution.py:334
  176.9 13.5 %collective-permute-done.19 = bf16[128,3584]{1,0:T(8,128)(2,1)} collective-permute-done((bf16[128,3584]{1,0:T(8,128)(2,1)}, bf16[128,3584]{1,0:T(8,128)(2,1)}, u32[]{:S(2)}, u32[]{:S(2)}) %collective-permute-start.19) | collective-permute-done | bytes 917536 | tf_op jit(solution)/shard_map/ppermute | solution.py:209
  190.4 1.4 collective-permute-start.30
  197.0 23.9 %collective-permute-done.21 = bf16[64,3584]{1,0:T(8,128)(2,1)S(1)} collective-permute-done((bf16[64,3584]{1,0:T(8,128)(2,1)S(1)}, bf16[64,3584]{1,0:T(8,128)(2,1)S(1)}, u32[]{:S(2)}, u32[]{:S(2)}) %collective-permute-start.21) | collective-permute-done | bytes 458784 | tf_op jit(solution)/shard_map/ppermute | solution.py:209
  221.6 11.1 %collective-permute-done.22 = bf16[64,3584]{1,0:T(8,128)(2,1)S(1)} collective-permute-done((bf16[64,3584]{1,0:T(8,128)(2,1)S(1)}, bf16[64,3584]{1,0:T(8,128)(2,1)S(1)}, u32[]{:S(2)}, u32[]{:S(2)}) %collective-permute-start.22) | collective-permute-done | bytes 458784 | tf_op jit(solution)/shard_map/ppermute | solution.py:209
  232.9 21.0 %shard_map.119 = bf16[3584,2048]{1,0:T(8,128)(2,1)} custom-call(s32[28,16]{1,0:T(8,128)S(1)} %copy.80.keep, bf16[512,3584]{1,0:T(8,128)(2,1)} %constant_dynamic-update-slice_fusion.10.m0, bf16[512,3584]{1,0:T(8,128)(2,1)} %collective-permute-done.28.m1, bf16[1024,2048]{1,0:T(8,128)(2,1)} %constant_dynamic-update-slice_fusion.15.grads), custom_call_target="tpu_custom_call" | custom-call | flops 15032385536 | bytes 22020096 | tf_op jit(solution)/shard_map/pallas_call | solution.py:150
  255.4 11.7 %collective-permute-done.32 = bf16[64,3584]{1,0:T(8,128)(2,1)S(1)} collective-permute-done((bf16[64,3584]{1,0:T(8,128)(2,1)S(1)}, bf16[64,3584]{1,0:T(8,128)(2,1)S(1)}, u32[]{:S(2)}, u32[]{:S(2)}) %collective-permute-start.32) | collective-permute-done | bytes 458784 | tf_op jit(solution)/shard_map/ppermute | solution.py:209
  267.9 1.9 constant_dynamic-update-slice_fusion
  269.9 2.0 copy-done.19
  271.9 20.5 %shard_map.120 = bf16[2048,3584]{1,0:T(8,128)(2,1)} custom-call(s32[16,28]{1,0:T(8,128)S(1)} %copy-done.13, bf16[2048,1024]{1,0:T(8,128)(2,1)} %bitcast.116, bf16[512,3584]{1,0:T(8,128)(2,1)S(1)} %constant_dynamic-update-slice_fusion.5.d0, bf16[512,3584]{1,0:T(8,128)(2,1)} %collective-permute-done.23.d1), custom_call_target="tpu_custom_call" | custom-call | flops 15032385536 | bytes 22020096 | tf_op jit(solution)/shard_map/pallas_call | solution.py:119
  292.3 20.5 %shard_map.121 = bf16[2048,3584]{1,0:T(8,128)(2,1)} custom-call(s32[16,28]{1,0:T(8,128)S(1)} %copy-done.14, bf16[2048,1024]{1,0:T(8,128)(2,1)} %bitcast.117, bf16[512,3584]{1,0:T(8,128)(2,1)S(1)} %constant_dynamic-update-slice_fusion.20.d0, bf16[512,3584]{1,0:T(8,128)(2,1)} %collective-permute-done.34.d1), custom_call_target="tpu_custom_call" | custom-call | flops 15032385536 | bytes 22020096 | tf_op jit(solution)/shard_map/pallas_call | solution.py:119
  (152 shorter events, 40.9 us)
Async XLA Ops:
  15.3 9.5 %copy-start.8 = (bf16[512,2048]{1,0:T(8,128)(2,1)S(1)}, bf16[512,2048]{1,0:T(8,128)(2,1)}, u32[]{:S(2)}) copy-start(bf16[512,2048]{1,0:T(8,128)(2,1)} %x.4) | copy-start | bytes 6291460
  15.3 9.5 %copy-start.14 = (s32[16,28]{1,0:T(8,128)S(1)}, s32[16,28]{1,0:T(8,128)}, u32[]{:S(2)}) copy-start(s32[16,28]{1,0:T(8,128)} %keep.7) | copy-start | bytes 5380
  18.2 45.5 %collective-permute-start.1 = (bf16[2,64,3584]{2,1,0:T(8,128)(2,1)}, bf16[2,64,3584]{2,1,0:T(8,128)(2,1)}, u32[]{:S(2)}, u32[]{:S(2)}) collective-permute-start(bf16[2,64,3584]{2,1,0:T(8,128)(2,1)} %dynamic-slice_bitcast_fusion.5), channel_id=1, source_target_pairs={{0,4},{4,0},{8,12},{12,8},{1,5},{5,1},{9,13},{13,9},{2,6},{6,2},{1... | collective-permute-start | bytes 2752520 | tf_op jit(solution)/shard_map/ppermute | solution.py:209
  23.3 42.0 %collective-permute-start.3 = (bf16[2,64,3584]{2,1,0:T(8,128)(2,1)}, bf16[2,64,3584]{2,1,0:T(8,128)(2,1)}, u32[]{:S(2)}, u32[]{:S(2)}) collective-permute-start(bf16[2,64,3584]{2,1,0:T(8,128)(2,1)} %dynamic-slice_bitcast_fusion.4), channel_id=1, source_target_pairs={{0,8},{4,12},{8,0},{12,4},{1,9},{5,13},{9,1},{13,5},{2,10},{6,14},... | collective-permute-start | bytes 2752520 | tf_op jit(solution)/shard_map/ppermute | solution.py:209
  38.2 30.3 %collective-permute-start.5 = (bf16[2,64,3584]{2,1,0:T(8,128)(2,1)}, bf16[2,64,3584]{2,1,0:T(8,128)(2,1)}, u32[]{:S(2)}, u32[]{:S(2)}) collective-permute-start(bf16[2,64,3584]{2,1,0:T(8,128)(2,1)} %dynamic-slice_bitcast_fusion.3), channel_id=1, source_target_pairs={{0,4},{4,0},{8,12},{12,8},{1,5},{5,1},{9,13},{13,9},{2,6},{6,2},{1... | collective-permute-start | bytes 2752520 | tf_op jit(solution)/shard_map/ppermute | solution.py:209
  40.5 28.9 %collective-permute-start.7 = (bf16[2,64,3584]{2,1,0:T(8,128)(2,1)}, bf16[2,64,3584]{2,1,0:T(8,128)(2,1)}, u32[]{:S(2)}, u32[]{:S(2)}) collective-permute-start(bf16[2,64,3584]{2,1,0:T(8,128)(2,1)} %dynamic-slice_bitcast_fusion.2), channel_id=1, source_target_pairs={{0,8},{4,12},{8,0},{12,4},{1,9},{5,13},{9,1},{13,5},{2,10},{6,14},... | collective-permute-start | bytes 2752520 | tf_op jit(solution)/shard_map/ppermute | solution.py:209
  41.1 16.4 %copy-start.21 = (s32[112]{0:T(128)S(1)}, s32[112]{0:T(128)}, u32[]{:S(2)}) copy-start(s32[112]{0:T(128)} %param.17) | copy-start | bytes 1348
  56.7 25.2 %collective-permute-start.12 = (bf16[2,64,3584]{2,1,0:T(8,128)(2,1)}, bf16[2,64,3584]{2,1,0:T(8,128)(2,1)}, u32[]{:S(2)}, u32[]{:S(2)}) collective-permute-start(bf16[2,64,3584]{2,1,0:T(8,128)(2,1)} %dynamic-slice_bitcast_fusion.1), channel_id=1, source_target_pairs={{0,4},{4,0},{8,12},{12,8},{1,5},{5,1},{9,13},{13,9},{2,6},{6,2},{1... | collective-permute-start | bytes 2752520 | tf_op jit(solution)/shard_map/ppermute | solution.py:209
  58.6 6.6 %copy-start.1 = (bf16[512,3584]{1,0:T(8,128)(2,1)S(1)}, bf16[512,3584]{1,0:T(8,128)(2,1)}, u32[]{:S(2)}) copy-start(bf16[512,3584]{1,0:T(8,128)(2,1)} %copy-done) | copy-start | bytes 11010052
  63.6 5.8 %copy-start.5 = (bf16[512,3584]{1,0:T(8,128)(2,1)S(1)}, bf16[512,3584]{1,0:T(8,128)(2,1)}, u32[]{:S(2)}) copy-start(bf16[512,3584]{1,0:T(8,128)(2,1)} %copy-done.4) | copy-start | bytes 11010052
  63.6 23.4 %collective-permute-start.14 = (bf16[2,64,3584]{2,1,0:T(8,128)(2,1)S(1)}, bf16[2,64,3584]{2,1,0:T(8,128)(2,1)S(1)}, u32[]{:S(2)}, u32[]{:S(2)}) collective-permute-start(bf16[2,64,3584]{2,1,0:T(8,128)(2,1)S(1)} %dynamic-slice_bitcast_fusion), channel_id=1, source_target_pairs={{0,8},{4,12},{8,0},{12,4},{1,9},{5,13},{9,1},{13,5},{2,10},{6,14},... | collective-permute-start | bytes 2752520 | tf_op jit(solution)/shard_map/ppermute | solution.py:209
  67.1 24.5 %collective-permute-start.4 = (bf16[64,3584]{1,0:T(8,128)(2,1)S(1)}, bf16[64,3584]{1,0:T(8,128)(2,1)S(1)}, u32[]{:S(2)}, u32[]{:S(2)}) collective-permute-start(bf16[64,3584]{1,0:T(8,128)(2,1)S(1)} %fusion.7), channel_id=1, source_target_pairs={{0,4},{4,0},{8,12},{12,8},{1,5},{5,1},{9,13},{13,9},{2,6},{6,2},{1... | collective-permute-start | bytes 1376264 | tf_op jit(solution)/shard_map/ppermute | solution.py:209
  68.5 18.5 %copy-start.3 = (bf16[512,3584]{1,0:T(8,128)(2,1)S(1)}, bf16[512,3584]{1,0:T(8,128)(2,1)}, u32[]{:S(2)}) copy-start(bf16[512,3584]{1,0:T(8,128)(2,1)} %copy-done.2) | copy-start | bytes 11010052
  68.5 28.3 %collective-permute-start.2 = (bf16[64,3584]{1,0:T(8,128)(2,1)S(1)}, bf16[64,3584]{1,0:T(8,128)(2,1)S(1)}, u32[]{:S(2)}, u32[]{:S(2)}) collective-permute-start(bf16[64,3584]{1,0:T(8,128)(2,1)S(1)} %fusion.6), channel_id=1, source_target_pairs={{0,8},{4,12},{8,0},{12,4},{1,9},{5,13},{9,1},{13,5},{2,10},{6,14},... | collective-permute-start | bytes 1376264 | tf_op jit(solution)/shard_map/ppermute | solution.py:209
  71.7 29.8 %collective-permute-start.8 = (bf16[64,3584]{1,0:T(8,128)(2,1)S(1)}, bf16[64,3584]{1,0:T(8,128)(2,1)S(1)}, u32[]{:S(2)}, u32[]{:S(2)}) collective-permute-start(bf16[64,3584]{1,0:T(8,128)(2,1)S(1)} %fusion.9), channel_id=1, source_target_pairs={{0,4},{4,0},{8,12},{12,8},{1,5},{5,1},{9,13},{13,9},{2,6},{6,2},{1... | collective-permute-start | bytes 1376264 | tf_op jit(solution)/shard_map/ppermute | solution.py:209
  81.9 24.7 %collective-permute-start.6 = (bf16[64,3584]{1,0:T(8,128)(2,1)S(1)}, bf16[64,3584]{1,0:T(8,128)(2,1)S(1)}, u32[]{:S(2)}, u32[]{:S(2)}) collective-permute-start(bf16[64,3584]{1,0:T(8,128)(2,1)S(1)} %fusion.8), channel_id=1, source_target_pairs={{0,8},{4,12},{8,0},{12,4},{1,9},{5,13},{9,1},{13,5},{2,10},{6,14},... | collective-permute-start | bytes 1376264 | tf_op jit(solution)/shard_map/ppermute | solution.py:209
  88.6 13.0 %copy-start.17 = (f32[2,64,3584]{2,1,0:T(8,128)}, f32[2,64,3584]{2,1,0:T(8,128)S(1)}, u32[]{:S(2)}) copy-start(f32[2,64,3584]{2,1,0:T(8,128)S(1)} %get-tuple-element.40) | copy-start | bytes 5505028
  88.6 23.9 %collective-permute-start.15 = (bf16[64,3584]{1,0:T(8,128)(2,1)S(1)}, bf16[64,3584]{1,0:T(8,128)(2,1)S(1)}, u32[]{:S(2)}, u32[]{:S(2)}) collective-permute-start(bf16[64,3584]{1,0:T(8,128)(2,1)S(1)} %fusion.11), channel_id=1, source_target_pairs={{0,4},{4,0},{8,12},{12,8},{1,5},{5,1},{9,13},{13,9},{2,6},{6,2},{1... | collective-permute-start | bytes 1376264 | tf_op jit(solution)/shard_map/ppermute | solution.py:209
  91.7 22.6 %collective-permute-start.13 = (bf16[64,3584]{1,0:T(8,128)(2,1)S(1)}, bf16[64,3584]{1,0:T(8,128)(2,1)}, u32[]{:S(2)}, u32[]{:S(2)}) collective-permute-start(bf16[64,3584]{1,0:T(8,128)(2,1)S(1)} %fusion.10), channel_id=1, source_target_pairs={{0,8},{4,12},{8,0},{12,4},{1,9},{5,13},{9,1},{13,5},{2,10},{6,14},... | collective-permute-start | bytes 1376264 | tf_op jit(solution)/shard_map/ppermute | solution.py:209
  106.7 5.8 %copy-start.18 = (f32[2,64,3584]{2,1,0:T(8,128)S(1)}, f32[2,64,3584]{2,1,0:T(8,128)}, u32[]{:S(2)}) copy-start(f32[2,64,3584]{2,1,0:T(8,128)} %copy-done.17) | copy-start | bytes 5505028
  107.3 7.0 %copy-start.16 = (f32[2,64,3584]{2,1,0:T(8,128)S(1)}, f32[2,64,3584]{2,1,0:T(8,128)}, u32[]{:S(2)}) copy-start(f32[2,64,3584]{2,1,0:T(8,128)} %copy-done.15) | copy-start | bytes 5505028
  108.1 9.9 %collective-permute-start.11 = (bf16[7,128,128]{2,1,0:T(8,128)(2,1)S(1)}, bf16[7,128,128]{2,1,0:T(8,128)(2,1)S(1)}, u32[]{:S(2)}, u32[]{:S(2)}) collective-permute-start(bf16[7,128,128]{2,1,0:T(8,128)(2,1)S(1)} %get-tuple-element.55), channel_id=1, source_target_pairs={{0,3},{1,2},{2,1},{3,0},{4,7},{5,6},{6,5},{7,4},{8,11},{9,10},{10,... | collective-permute-start | bytes 688136 | tf_op jit(solution)/shard_map/ppermute | solution.py:209
  111.8 15.1 %collective-permute-start.10 = (bf16[7,128,128]{2,1,0:T(8,128)(2,1)S(1)}, bf16[7,128,128]{2,1,0:T(8,128)(2,1)S(1)}, u32[]{:S(2)}, u32[]{:S(2)}) collective-permute-start(bf16[7,128,128]{2,1,0:T(8,128)(2,1)S(1)} %get-tuple-element.56), channel_id=1, source_target_pairs={{0,2},{1,3},{2,0},{3,1},{4,6},{5,7},{6,4},{7,5},{8,10},{9,11},{10,... | collective-permute-start | bytes 688136 | tf_op jit(solution)/shard_map/ppermute | solution.py:209
  111.8 15.1 %collective-permute-start.9 = (bf16[7,128,128]{2,1,0:T(8,128)(2,1)S(1)}, bf16[7,128,128]{2,1,0:T(8,128)(2,1)S(1)}, u32[]{:S(2)}, u32[]{:S(2)}) collective-permute-start(bf16[7,128,128]{2,1,0:T(8,128)(2,1)S(1)} %get-tuple-element.57), channel_id=1, source_target_pairs={{0,1},{1,0},{2,3},{3,2},{4,5},{5,4},{6,7},{7,6},{8,9},{9,8},{10,11... | collective-permute-start | bytes 688136 | tf_op jit(solution)/shard_map/ppermute | solution.py:209
  127.6 24.9 %collective-permute-start.25 = (bf16[128,3584]{1,0:T(8,128)(2,1)S(1)}, bf16[128,3584]{1,0:T(8,128)(2,1)S(1)}, u32[]{:S(2)}, u32[]{:S(2)}) collective-permute-start(bf16[128,3584]{1,0:T(8,128)(2,1)S(1)} %shard_map.116), channel_id=1, source_target_pairs={{0,8},{4,12},{8,0},{12,4},{1,9},{5,13},{9,1},{13,5},{2,10},{6,14},... | collective-permute-start | bytes 2752520 | tf_op jit(solution)/shard_map/ppermute | solution.py:209
  129.2 24.1 %collective-permute-start.24 = (bf16[128,3584]{1,0:T(8,128)(2,1)S(1)}, bf16[128,3584]{1,0:T(8,128)(2,1)S(1)}, u32[]{:S(2)}, u32[]{:S(2)}) collective-permute-start(bf16[128,3584]{1,0:T(8,128)(2,1)S(1)} %shard_map.116), channel_id=1, source_target_pairs={{0,4},{4,0},{8,12},{12,8},{1,5},{5,1},{9,13},{13,9},{2,6},{6,2},{1... | collective-permute-start | bytes 2752520 | tf_op jit(solution)/shard_map/ppermute | solution.py:209
  130.6 10.5 %collective-permute-start.18 = (bf16[7,128,128]{2,1,0:T(8,128)(2,1)S(1)}, bf16[7,128,128]{2,1,0:T(8,128)(2,1)S(1)}, u32[]{:S(2)}, u32[]{:S(2)}) collective-permute-start(bf16[7,128,128]{2,1,0:T(8,128)(2,1)S(1)} %get-tuple-element.51), channel_id=1, source_target_pairs={{0,3},{1,2},{2,1},{3,0},{4,7},{5,6},{6,5},{7,4},{8,11},{9,10},{10,... | collective-permute-start | bytes 688136 | tf_op jit(solution)/shard_map/ppermute | solution.py:209
  133.2 17.4 %collective-permute-start.17 = (bf16[7,128,128]{2,1,0:T(8,128)(2,1)S(1)}, bf16[7,128,128]{2,1,0:T(8,128)(2,1)S(1)}, u32[]{:S(2)}, u32[]{:S(2)}) collective-permute-start(bf16[7,128,128]{2,1,0:T(8,128)(2,1)S(1)} %get-tuple-element.52), channel_id=1, source_target_pairs={{0,2},{1,3},{2,0},{3,1},{4,6},{5,7},{6,4},{7,5},{8,10},{9,11},{10,... | collective-permute-start | bytes 688136 | tf_op jit(solution)/shard_map/ppermute | solution.py:209
  133.2 17.4 %collective-permute-start.16 = (bf16[7,128,128]{2,1,0:T(8,128)(2,1)S(1)}, bf16[7,128,128]{2,1,0:T(8,128)(2,1)S(1)}, u32[]{:S(2)}, u32[]{:S(2)}) collective-permute-start(bf16[7,128,128]{2,1,0:T(8,128)(2,1)S(1)} %get-tuple-element.53), channel_id=1, source_target_pairs={{0,1},{1,0},{2,3},{3,2},{4,5},{5,4},{6,7},{7,6},{8,9},{9,8},{10,11... | collective-permute-start | bytes 688136 | tf_op jit(solution)/shard_map/ppermute | solution.py:209
  141.1 31.1 %collective-permute-start.29 = (bf16[512,2048]{1,0:T(8,128)(2,1)}, bf16[512,2048]{1,0:T(8,128)(2,1)}, u32[]{:S(2)}, u32[]{:S(2)}) collective-permute-start(bf16[512,2048]{1,0:T(8,128)(2,1)} %pad_maximum_fusion.1), channel_id=1, source_target_pairs={{0,16},{16,0},{1,17},{17,1},{2,18},{18,2},{3,19},{19,3},{4,20},{20... | collective-permute-start | bytes 6291464 | tf_op jit(solution)/shard_map/ppermute | solution.py:209
  152.5 11.7 %collective-permute-start.27 = (bf16[64,3584]{1,0:T(8,128)(2,1)S(1)}, bf16[64,3584]{1,0:T(8,128)(2,1)S(1)}, u32[]{:S(2)}, u32[]{:S(2)}) collective-permute-start(bf16[64,3584]{1,0:T(8,128)(2,1)S(1)} %slice.67), channel_id=1, source_target_pairs={{0,4},{4,0},{8,12},{12,8},{1,5},{5,1},{9,13},{13,9},{2,6},{6,2},{1... | collective-permute-start | bytes 1376264 | tf_op jit(solution)/shard_map/ppermute | solution.py:209
  153.3 10.2 %collective-permute-start.26 = (bf16[64,3584]{1,0:T(8,128)(2,1)S(1)}, bf16[64,3584]{1,0:T(8,128)(2,1)S(1)}, u32[]{:S(2)}, u32[]{:S(2)}) collective-permute-start(bf16[64,3584]{1,0:T(8,128)(2,1)S(1)} %slice.66), channel_id=1, source_target_pairs={{0,8},{4,12},{8,0},{12,4},{1,9},{5,13},{9,1},{13,5},{2,10},{6,14},... | collective-permute-start | bytes 1376264 | tf_op jit(solution)/shard_map/ppermute | solution.py:209
  165.0 4.2 %copy-start.9 = (bf16[512,2048]{1,0:T(8,128)(2,1)S(1)}, bf16[512,2048]{1,0:T(8,128)(2,1)}, u32[]{:S(2)}) copy-start(bf16[512,2048]{1,0:T(8,128)(2,1)} %x.4) | copy-start | bytes 6291460
  165.0 67.8 %collective-permute-start.28 = (bf16[512,3584]{1,0:T(8,128)(2,1)}, bf16[512,3584]{1,0:T(8,128)(2,1)}, u32[]{:S(2)}, u32[]{:S(2)}) collective-permute-start(bf16[512,3584]{1,0:T(8,128)(2,1)} %constant_dynamic-update-slice_fusion.10.m0), channel_id=1, source_target_pairs={{0,16},{16,0},{1,17},{17,1},{2,18},{18,2},{3,19},{19,3},{4,20},{20... | collective-permute-start | bytes 11010056 | tf_op jit(solution)/shard_map/ppermute | solution.py:209
  167.4 23.1 %collective-permute-start.19 = (bf16[128,3584]{1,0:T(8,128)(2,1)}, bf16[128,3584]{1,0:T(8,128)(2,1)}, u32[]{:S(2)}, u32[]{:S(2)}) collective-permute-start(bf16[128,3584]{1,0:T(8,128)(2,1)} %get-tuple-element.46), channel_id=1, source_target_pairs={{0,4},{4,0},{8,12},{12,8},{1,5},{5,1},{9,13},{13,9},{2,6},{6,2},{1... | collective-permute-start | bytes 2752520 | tf_op jit(solution)/shard_map/ppermute | solution.py:209
  168.7 24.1 %collective-permute-start.20 = (bf16[128,3584]{1,0:T(8,128)(2,1)}, bf16[128,3584]{1,0:T(8,128)(2,1)}, u32[]{:S(2)}, u32[]{:S(2)}) collective-permute-start(bf16[128,3584]{1,0:T(8,128)(2,1)} %get-tuple-element.46), channel_id=1, source_target_pairs={{0,8},{4,12},{8,0},{12,4},{1,9},{5,13},{9,1},{13,5},{2,10},{6,14},... | collective-permute-start | bytes 2752520 | tf_op jit(solution)/shard_map/ppermute | solution.py:209
  172.1 95.8 %collective-permute-start = (bf16[512,2048]{0,1:T(8,128)(2,1)}, bf16[512,2048]{0,1:T(8,128)(2,1)}, u32[]{:S(2)}, u32[]{:S(2)}) collective-permute-start(bf16[512,2048]{0,1:T(8,128)(2,1)} %pad_maximum_fusion), channel_id=1, source_target_pairs={{0,16},{16,0},{1,17},{17,1},{2,18},{18,2},{3,19},{19,3},{4,20},{20... | collective-permute-start | bytes 6291464 | tf_op jit(solution)/shard_map/ppermute | solution.py:209
  172.2 22.3 %copy-start.11 = (bf16[512,3584]{1,0:T(8,128)(2,1)S(1)}, bf16[512,3584]{1,0:T(8,128)(2,1)}, u32[]{:S(2)}) copy-start(bf16[512,3584]{1,0:T(8,128)(2,1)} %get-tuple-element.45) | copy-start | bytes 11010052
  172.2 81.7 %collective-permute-start.31 = (bf16[128,3584]{1,0:T(8,128)(2,1)S(1)}, bf16[128,3584]{1,0:T(8,128)(2,1)S(1)}, u32[]{:S(2)}, u32[]{:S(2)}) collective-permute-start(bf16[128,3584]{1,0:T(8,128)(2,1)S(1)} %get-tuple-element.26), channel_id=1, source_target_pairs={{0,8},{4,12},{8,0},{12,4},{1,9},{5,13},{9,1},{13,5},{2,10},{6,14},... | collective-permute-start | bytes 2752520 | tf_op jit(solution)/shard_map/ppermute | solution.py:209
  190.4 63.5 %collective-permute-start.30 = (bf16[128,3584]{1,0:T(8,128)(2,1)S(1)}, bf16[128,3584]{1,0:T(8,128)(2,1)S(1)}, u32[]{:S(2)}, u32[]{:S(2)}) collective-permute-start(bf16[128,3584]{1,0:T(8,128)(2,1)S(1)} %get-tuple-element.26), channel_id=1, source_target_pairs={{0,4},{4,0},{8,12},{12,8},{1,5},{5,1},{9,13},{13,9},{2,6},{6,2},{1... | collective-permute-start | bytes 2752520 | tf_op jit(solution)/shard_map/ppermute | solution.py:209
  192.9 28.0 %collective-permute-start.21 = (bf16[64,3584]{1,0:T(8,128)(2,1)S(1)}, bf16[64,3584]{1,0:T(8,128)(2,1)S(1)}, u32[]{:S(2)}, u32[]{:S(2)}) collective-permute-start(bf16[64,3584]{1,0:T(8,128)(2,1)S(1)} %slice.64), channel_id=1, source_target_pairs={{0,8},{4,12},{8,0},{12,4},{1,9},{5,13},{9,1},{13,5},{2,10},{6,14},... | collective-permute-start | bytes 1376264 | tf_op jit(solution)/shard_map/ppermute | solution.py:209
  220.9 11.8 %collective-permute-start.22 = (bf16[64,3584]{1,0:T(8,128)(2,1)S(1)}, bf16[64,3584]{1,0:T(8,128)(2,1)S(1)}, u32[]{:S(2)}, u32[]{:S(2)}) collective-permute-start(bf16[64,3584]{1,0:T(8,128)(2,1)S(1)} %slice.65), channel_id=1, source_target_pairs={{0,4},{4,0},{8,12},{12,8},{1,5},{5,1},{9,13},{13,9},{2,6},{6,2},{1... | collective-permute-start | bytes 1376264 | tf_op jit(solution)/shard_map/ppermute | solution.py:209
  232.8 21.1 %copy-start.10 = (bf16[512,3584]{1,0:T(8,128)(2,1)S(1)}, bf16[512,3584]{1,0:T(8,128)(2,1)}, u32[]{:S(2)}) copy-start(bf16[512,3584]{1,0:T(8,128)(2,1)} %get-tuple-element.25) | copy-start | bytes 11010052
  232.8 37.1 %collective-permute-start.23 = (bf16[512,3584]{1,0:T(8,128)(2,1)S(1)}, bf16[512,3584]{1,0:T(8,128)(2,1)}, u32[]{:S(2)}, u32[]{:S(2)}) collective-permute-start(bf16[512,3584]{1,0:T(8,128)(2,1)S(1)} %constant_dynamic-update-slice_fusion.5.d0), channel_id=1, source_target_pairs={{0,16},{16,0},{1,17},{17,1},{2,18},{18,2},{3,19},{19,3},{4,20},{20... | collective-permute-start | bytes 11010056 | tf_op jit(solution)/shard_map/ppermute | solution.py:209
  254.1 13.0 %collective-permute-start.33 = (bf16[64,3584]{1,0:T(8,128)(2,1)S(1)}, bf16[64,3584]{1,0:T(8,128)(2,1)S(1)}, u32[]{:S(2)}, u32[]{:S(2)}) collective-permute-start(bf16[64,3584]{1,0:T(8,128)(2,1)S(1)} %slice.55), channel_id=1, source_target_pairs={{0,4},{4,0},{8,12},{12,8},{1,5},{5,1},{9,13},{13,9},{2,6},{6,2},{1... | collective-permute-start | bytes 1376264 | tf_op jit(solution)/shard_map/ppermute | solution.py:209
  254.8 12.3 %collective-permute-start.32 = (bf16[64,3584]{1,0:T(8,128)(2,1)S(1)}, bf16[64,3584]{1,0:T(8,128)(2,1)S(1)}, u32[]{:S(2)}, u32[]{:S(2)}) collective-permute-start(bf16[64,3584]{1,0:T(8,128)(2,1)S(1)} %slice.54), channel_id=1, source_target_pairs={{0,8},{4,12},{8,0},{12,4},{1,9},{5,13},{9,1},{13,5},{2,10},{6,14},... | collective-permute-start | bytes 1376264 | tf_op jit(solution)/shard_map/ppermute | solution.py:209
  267.1 25.2 %collective-permute-start.34 = (bf16[512,3584]{1,0:T(8,128)(2,1)S(1)}, bf16[512,3584]{1,0:T(8,128)(2,1)}, u32[]{:S(2)}, u32[]{:S(2)}) collective-permute-start(bf16[512,3584]{1,0:T(8,128)(2,1)S(1)} %constant_dynamic-update-slice_fusion.20.d0), channel_id=1, source_target_pairs={{0,16},{16,0},{1,17},{17,1},{2,18},{18,2},{3,19},{19,3},{4,20},{20... | collective-permute-start | bytes 11010056 | tf_op jit(solution)/shard_map/ppermute | solution.py:209
  267.4 4.5 %copy-start.13 = (s32[16,28]{1,0:T(8,128)S(1)}, s32[16,28]{1,0:T(8,128)}, u32[]{:S(2)}) copy-start(s32[16,28]{1,0:T(8,128)} %keep.6) | copy-start | bytes 5380
  (9 other events, 21.2 us)

commit v3 on v2

--- a/solution.py
+++ b/solution.py
@@ -99,11 +99,17 @@
             ).astype(BF16)
 
 
-def in_grad_kernel(tb, strip, keep, xt, d0, d1, out, both):
+def stack(both, pieces):
+    at = 0
+    for piece in pieces:
+        both[at : at + piece.shape[0]] = piece[...]
+        at += piece.shape[0]
+
+
+def in_grad_kernel(tb, strip, keep, xt, *refs):
+    *pieces, out, both = refs
     col0 = pl.program_id(0) * tb
-    half = d0.shape[0]
-    both[:half] = d0[...]
-    both[half:] = d1[...]
+    stack(both, pieces)
     for base in range(0, xt.shape[0], strip):
         value = lax.dot_general(
             xt[base : base + strip], both[...], NN, preferred_element_type=F32
@@ -111,9 +117,9 @@
         store_masked(out, value, keep, base // BLK, col0, base)
 
 
-def in_grad(xt, d0, d1, keep):
+def in_grad(xt, pieces, keep):
     rows, depth = xt.shape
-    half, cols = d0.shape
+    cols = pieces[0].shape[1]
     tb = tile_blocks(cols // BLK)
     tn = tb * BLK
     return pl.pallas_call(
@@ -123,28 +129,26 @@
         in_specs=[
             pl.BlockSpec(memory_space=pltpu.SMEM),
             pl.BlockSpec((rows, depth), lambda j: (0, 0)),
-            pl.BlockSpec((half, tn), lambda j: (0, j)),
-            pl.BlockSpec((half, tn), lambda j: (0, j)),
-        ],
+        ]
+        + [pl.BlockSpec((p.shape[0], tn), lambda j: (0, j)) for p in pieces],
         out_specs=pl.BlockSpec((rows, tn), lambda j: (0, j)),
-        scratch_shapes=[pltpu.VMEM((2 * half, tn), BF16)],
+        scratch_shapes=[pltpu.VMEM((depth, tn), BF16)],
         compiler_params=params(),
         cost_estimate=cost(rows, depth, cols, 2 * depth * cols + 2 * rows * cols),
-    )(keep, xt, d0, d1)
-
-
-def out_grad_kernel(tb, keep, m0, m1, grads, out, both):
+    )(keep, xt, *pieces)
+
+
+def out_grad_kernel(tb, keep, grads, *refs):
+    *pieces, out, both = refs
     row0 = pl.program_id(0) * tb
-    half = m0.shape[0]
-    both[:half] = m0[...]
-    both[half:] = m1[...]
+    stack(both, pieces)
     value = lax.dot_general(both[...], grads[...], TN, preferred_element_type=F32)
     store_masked(out, value, keep, row0, 0, 0)
 
 
-def down_grad(m0, m1, grads, keep):
-    half, rows = m0.shape
-    cols = grads.shape[1]
+def down_grad(pieces, grads, keep):
+    rows = pieces[0].shape[1]
+    depth, cols = grads.shape
     tb = tile_blocks(rows // BLK)
     tm = tb * BLK
     return pl.pallas_call(
@@ -153,15 +157,14 @@
         out_shape=jax.ShapeDtypeStruct((rows, cols), BF16),
         in_specs=[
             pl.BlockSpec(memory_space=pltpu.SMEM),
-            pl.BlockSpec((half, tm), lambda j: (0, j)),
-            pl.BlockSpec((half, tm), lambda j: (0, j)),
-            pl.BlockSpec((2 * half, cols), lambda j: (0, 0)),
-        ],
+            pl.BlockSpec((depth, cols), lambda j: (0, 0)),
+        ]
+        + [pl.BlockSpec((p.shape[0], tm), lambda j: (0, j)) for p in pieces],
         out_specs=pl.BlockSpec((tm, cols), lambda j: (j, 0)),
-        scratch_shapes=[pltpu.VMEM((2 * half, tm), BF16)],
-        compiler_params=params(),
-        cost_estimate=cost(rows, 2 * half, cols, 4 * half * rows + 2 * rows * cols),
-    )(keep, m0, m1, grads)
+        scratch_shapes=[pltpu.VMEM((depth, tm), BF16)],
+        compiler_params=params(),
+        cost_estimate=cost(rows, depth, cols, 2 * depth * rows + 2 * rows * cols),
+    )(keep, grads, *pieces)
 
 
 def pick_kernel(idx, x, out):
@@ -258,6 +261,12 @@
     return [own, one, two, swap(one[:piece], "mp", n, 2), swap(two[piece:], "mp", n, 1)]
 
 
+def both_groups(pieces, n_dp):
+    early, late = pieces[:3], pieces[3:]
+    other = [swap(jnp.concatenate(part, 0), "dp", n_dp, 1) for part in (early, late) if part]
+    return pieces + other
+
+
 def gathered_order(x, n, me):
     split = x.reshape(n, x.shape[0] // n, x.shape[1])
     return jnp.concatenate(
@@ -334,14 +343,13 @@
     grd = jnp.concatenate([grd, swap(grd, "dp", n_dp, 1)], 0)
     tok_t = jnp.concatenate([tok, swap(tok, "dp", n_dp, 1)], 0).T
 
-    moved_all = jnp.concatenate(gather_pieces(moved, n_mp), 0)
-    down = down_grad(moved_all, swap(moved_all, "dp", n_dp, 1), grd, down_keep)
-    gate_all = jnp.concatenate(gather_pieces(gate_delta, n_mp), 0)
-    gate_other = after(down, swap(gate_all, "dp", n_dp, 1))
-    gate_grad = in_grad(tok_t, gate_all, gate_other, gate_keep)
-    up_all = jnp.concatenate(gather_pieces(up_delta, n_mp, down), 0)
-    up_other = after(gate_grad, swap(up_all, "dp", n_dp, 1))
-    up_grad = in_grad(tok_t, up_all, up_other, up_keep)
+    down = down_grad(both_groups(gather_pieces(moved, n_mp), n_dp), grd, down_keep)
+    gate_pieces = gather_pieces(gate_delta, n_mp)
+    gate_pieces[3:] = after(down, gate_pieces[3:])
+    gate_grad = in_grad(tok_t, both_groups(gate_pieces, n_dp), gate_keep)
+    up_pieces = gather_pieces(up_delta, n_mp, down)
+    up_pieces[3:] = after(gate_grad, up_pieces[3:])
+    up_grad = in_grad(tok_t, both_groups(up_pieces, n_dp), up_keep)
     return gate_grad, up_grad, down
 
 

time: 314 us -> 306 us (0.975)
  waiting for transfers between devices: 120 us -> 97.8 us
  local copies, waits for them, and re-layouts: 37.3 us -> 43.3 us
  other arithmetic: 15.2 us -> 21 us
    ppermute x35 -> x38, waiting for transfers between devices: 120 us -> 97.8 us  [swap(): return lax.ppermute(x, axis, [(i, i ^ bits) for i in range(n)])]
    concatenate x0 -> x6, other arithmetic: none -> 5.99 us  [both_groups(): jnp.concatenate(part, 0)]
    unnamed x67 -> x83, local copies, waits for them, and re-layouts: 20.6 us -> 22.6 us
    ppermute x35 -> x38, starting transfers between devices: 36.9 us -> 38.5 us  [swap(): return lax.ppermute(x, axis, [(i, i ^ bits) for i in range(n)])]
  transfers between devices with their start and end apart: 35 -> 38, of which waited for: 16 -> 14; matrix products, arithmetic and copies ran while one was open for 14% -> 18% of each run, Pallas kernels for 22% -> 23%
where the time goes in v3:
time: 306 us; the launch traced here: 305 us
  Pallas kernels  103 us (34%)
  waiting for transfers between devices  97.8 us (32%)
  local copies, waits for them, and re-layouts  43.3 us (14%)
  starting transfers between devices  38.5 us (13%)
  other arithmetic  21 us (7%)
    ppermute x38, waiting for transfers between devices, swap(): return lax.ppermute(x, axis, [(i, i ^ bits) for i in range(n)])  97.8 us
    pallas_call x2, Pallas kernels, in_grad(): pl.pallas_call(functools.partial(in_grad_kernel, tb, min(512, rows)), gri...  41.4 us
    ppermute x38, starting transfers between devices, swap(): return lax.ppermute(x, axis, [(i, i ^ bits) for i in range(n)])  38.5 us
    pallas_call x2, Pallas kernels, times_columns(): pl.pallas_call(functools.partial(columns_kernel, tb), grid=(cols // tn,),...  24.7 us
    unnamed x83, local copies, waits for them, and re-layouts  22.6 us
    pallas_call x1, Pallas kernels, down_grad(): pl.pallas_call(functools.partial(out_grad_kernel, tb), grid=(rows // tm,)...  21 us
    pallas_call x1, Pallas kernels, times_rows(): pl.pallas_call(functools.partial(rows_kernel, tb), grid=(cols // tn,), ou...  12.7 us
    reshape x6, local copies, waits for them, and re-layouts, scatter_sum(): sent = lax.dynamic_slice(split, start, size).reshape(shape)  8.34 us
  transfers between devices with their start and end apart: 38, of which 14 were waited for; matrix products, arithmetic and copies ran while one was open for 18% of the time, Pallas kernels for 23%

profile of v3, /device:TPU:0, one launch (start us, length us, event | category | flops | bytes accessed | tf_op | source)
XLA Modules:
  0.0 304.6 jit_solution(10924363251684512043)
XLA Ops:
  0.7 1.6 copy-done.7
  2.9 12.3 %shard_map.112 = bf16[512,3584]{1,0:T(8,128)(2,1)S(1)} custom-call(s32[16,28]{1,0:T(8,128)S(1)} %copy-done.13, bf16[512,2048]{1,0:T(8,128)(2,1)S(1)} %copy-done.7, bf16[2048,3584]{1,0:T(8,128)(2,1)} %w.3), custom_call_target="tpu_custom_call" | custom-call | flops 7516192768 | bytes 18350080 | tf_op jit(solution)/shard_map/pallas_call | solution.py:55
  15.3 1.8 copy-done
  18.1 2.9 collective-permute-start.1
  21.1 2.2 dynamic-slice_bitcast_fusion.4
  23.2 1.5 collective-permute-start.3
  24.8 12.3 %shard_map.113 = bf16[512,3584]{1,0:T(8,128)(2,1)S(1)} custom-call(s32[16,28]{1,0:T(8,128)S(1)} %copy-done.15, bf16[512,2048]{1,0:T(8,128)(2,1)S(1)} %copy-done.8, bf16[2048,3584]{1,0:T(8,128)(2,1)} %w.4), custom_call_target="tpu_custom_call" | custom-call | flops 7516192768 | bytes 18350080 | tf_op jit(solution)/shard_map/pallas_call | solution.py:55
  41.0 12.7 %shard_map.114 = bf16[512,3584]{1,0:T(8,128)(2,1)S(1)} custom-call(s32[28,16]{1,0:T(8,128)S(1)} %copy.66.keep, bf16[512,2048]{1,0:T(8,128)(2,1)S(1)} %copy-done.6, bf16[3584,2048]{1,0:T(8,128)(2,1)} %w.5), custom_call_target="tpu_custom_call" | custom-call | flops 7516192768 | bytes 18350080 | tf_op jit(solution)/shard_map/pallas_call | solution.py:76
  53.7 1.8 copy-done.2
  57.3 2.2 dynamic-slice_bitcast_fusion
  60.6 2.7 constant_dynamic-slice_fusion.2
  64.7 2.3 copy.81
  72.5 3.3 %pad_maximum_fusion.4 = bf16[512,2048]{1,0:T(8,128)(2,1)} fusion(bf16[128,2048]{1,0:T(8,128)(2,1)} %get-tuple-element.30, bf16[128,2048]{1,0:T(8,128)(2,1)} %get-tuple-element.32, bf16[128,2048]{1,0:T(8,128)(2,1)} %get-tuple-element.34, bf16[128,2048]{1,0:T(8,128)(2,1)} %get-tuple-element.36), kind=kLoop, calls=%fused_computation.6 | loop fusion | flops 8388608 | bytes 4194304 | tf_op jit(solution)/shard_map/concatenate | solution.py:272
  77.5 1.5 collective-permute-start.14
  79.0 2.1 convert_add_fusion.5
  83.1 2.1 convert_add_fusion.3
  86.2 14.5 %collective-permute-done.14 = bf16[2,64,3584]{2,1,0:T(8,128)(2,1)S(1)} collective-permute-done((bf16[2,64,3584]{2,1,0:T(8,128)(2,1)S(1)}, bf16[2,64,3584]{2,1,0:T(8,128)(2,1)S(1)}, u32[]{:S(2)}, u32[]{:S(2)}) %collective-permute-start.14) | collective-permute-done | bytes 917536 | tf_op jit(solution)/shard_map/ppermute | solution.py:212
  100.8 1.5 collective-permute-start.6
  102.3 1.7 convert_add_fusion.1
  105.6 5.0 %collective-permute-done.2 = bf16[64,3584]{1,0:T(8,128)(2,1)S(1)} collective-permute-done((bf16[64,3584]{1,0:T(8,128)(2,1)S(1)}, bf16[64,3584]{1,0:T(8,128)(2,1)S(1)}, u32[]{:S(2)}, u32[]{:S(2)}) %collective-permute-start.2) | collective-permute-done | bytes 458784 | tf_op jit(solution)/shard_map/ppermute | solution.py:212
  110.6 1.5 collective-permute-start.13
  112.4 8.1 %collective-permute-done.6 = bf16[64,3584]{1,0:T(8,128)(2,1)S(1)} collective-permute-done((bf16[64,3584]{1,0:T(8,128)(2,1)S(1)}, bf16[64,3584]{1,0:T(8,128)(2,1)S(1)}, u32[]{:S(2)}, u32[]{:S(2)}) %collective-permute-start.6) | collective-permute-done | bytes 458784 | tf_op jit(solution)/shard_map/ppermute | solution.py:212
  122.3 3.7 %collective-permute-start.11 = (bf16[7,128,128]{2,1,0:T(8,128)(2,1)S(1)}, bf16[7,128,128]{2,1,0:T(8,128)(2,1)S(1)}, u32[]{:S(2)}, u32[]{:S(2)}) collective-permute-start(bf16[7,128,128]{2,1,0:T(8,128)(2,1)S(1)} %get-tuple-element.55), channel_id=1, source_target_pairs={{0,3},{1,2},{2,1},{3,0},{4,7},{5,6},{6,5},{7,4},{8,11},{9,10},{10,... | collective-permute-start | bytes 688136 | tf_op jit(solution)/shard_map/ppermute | solution.py:212
  126.9 5.1 %collective-permute-done.11.refs_3_ = bf16[7,128,128]{2,1,0:T(8,128)(2,1)S(1)} collective-permute-done((bf16[7,128,128]{2,1,0:T(8,128)(2,1)S(1)}, bf16[7,128,128]{2,1,0:T(8,128)(2,1)S(1)}, u32[]{:S(2)}, u32[]{:S(2)}) %collective-permute-start.11) | collective-permute-done | bytes 229408 | tf_op jit(solution)/shard_map/ppermute | solution.py:212
  131.9 8.7 %collective-permute-done.10.refs_2_ = bf16[7,128,128]{2,1,0:T(8,128)(2,1)S(1)} collective-permute-done((bf16[7,128,128]{2,1,0:T(8,128)(2,1)S(1)}, bf16[7,128,128]{2,1,0:T(8,128)(2,1)S(1)}, u32[]{:S(2)}, u32[]{:S(2)}) %collective-permute-start.10) | collective-permute-done | bytes 229408 | tf_op jit(solution)/shard_map/ppermute | solution.py:212
  141.4 1.6 collective-permute-start.25
  143.0 1.7 collective-permute-start.24
  144.9 2.0 copy.83
  148.6 2.5 collective-permute-start.18
  151.0 11.7 %collective-permute-done.25.refs_2_ = bf16[128,3584]{1,0:T(8,128)(2,1)S(1)} collective-permute-done((bf16[128,3584]{1,0:T(8,128)(2,1)S(1)}, bf16[128,3584]{1,0:T(8,128)(2,1)S(1)}, u32[]{:S(2)}, u32[]{:S(2)}) %collective-permute-start.25) | collective-permute-done | bytes 917536 | tf_op jit(solution)/shard_map/ppermute | solution.py:212
  162.8 1.4 collective-permute-done.24.refs_1_
  164.2 2.9 pad_maximum_fusion
  169.1 3.3 %collective-permute-done.16.refs_1_ = bf16[7,128,128]{2,1,0:T(8,128)(2,1)S(1)} collective-permute-done((bf16[7,128,128]{2,1,0:T(8,128)(2,1)S(1)}, bf16[7,128,128]{2,1,0:T(8,128)(2,1)S(1)}, u32[]{:S(2)}, u32[]{:S(2)}) %collective-permute-start.16) | collective-permute-done | bytes 229408 | tf_op jit(solution)/shard_map/ppermute | solution.py:212
  178.9 5.9 %collective-permute-done.27.refs_4_ = bf16[64,3584]{1,0:T(8,128)(2,1)S(1)} collective-permute-done((bf16[64,3584]{1,0:T(8,128)(2,1)S(1)}, bf16[64,3584]{1,0:T(8,128)(2,1)S(1)}, u32[]{:S(2)}, u32[]{:S(2)}) %collective-permute-start.27) | collective-permute-done | bytes 458784 | tf_op jit(solution)/shard_map/ppermute | solution.py:212
  184.8 1.7 collective-permute-start.19
  186.5 2.5 collective-permute-done.26.refs_3_
  190.9 1.6 pad_maximum_fusion.3
  193.0 3.2 %constant_dynamic-update-slice_fusion.5.grads = bf16[1024,2048]{1,0:T(8,128)(2,1)} fusion(bf16[1024,2048]{1,0:T(8,128)(2,1)} %get-tuple-element.29, bf16[512,2048]{1,0:T(8,128)(2,1)} %collective-permute-done.23), kind=kLoop, calls=%fused_computation.65 | loop fusion | bytes 4194304 | tf_op jit(solution)/shard_map/concatenate | solution.py:343
  196.2 10.9 %collective-permute-done.20.refs_2_ = bf16[128,3584]{1,0:T(8,128)(2,1)} collective-permute-done((bf16[128,3584]{1,0:T(8,128)(2,1)S(1)}, bf16[128,3584]{1,0:T(8,128)(2,1)}, u32[]{:S(2)}, u32[]{:S(2)}) %collective-permute-start.20) | collective-permute-done | bytes 917536 | tf_op jit(solution)/shard_map/ppermute | solution.py:212
  210.9 1.7 pad_maximum_fusion.1
  213.5 21.0 %shard_map.119 = bf16[3584,2048]{1,0:T(8,128)(2,1)} custom-call(s32[28,16]{1,0:T(8,128)S(1)} %copy.80.keep, bf16[1024,2048]{1,0:T(8,128)(2,1)} %constant_dynamic-update-slice_fusion.5.grads, bf16[128,3584]{1,0:T(8,128)(2,1)S(1)} %shard_map.116.refs_0_, bf16[128,3584]{1,0:T(8,128)(2,1)} %collective-permute-done.24.refs_1_, bf16[128,3584]{1,0:T(8,128)(2,1)S(1)} %copy-done.10, ...), custom_call_target="tpu_custom_call" | custom-call | flops 15032385536 | bytes 22020096 | tf_op jit(solution)/shard_map/pallas_call | solution.py:154
  234.5 1.8 collective-permute-start.32
  238.6 1.6 constant_dynamic-update-slice_fusion
  240.2 17.1 %collective-permute-done.32.refs_1_ = bf16[128,3584]{1,0:T(8,128)(2,1)S(1)} collective-permute-done((bf16[128,3584]{1,0:T(8,128)(2,1)S(1)}, bf16[128,3584]{1,0:T(8,128)(2,1)S(1)}, u32[]{:S(2)}, u32[]{:S(2)}) %collective-permute-start.32) | collective-permute-done | bytes 917536 | tf_op jit(solution)/shard_map/ppermute | solution.py:212
  257.4 1.8 collective-permute-start.35
  260.5 20.7 %shard_map.120 = bf16[2048,3584]{1,0:T(8,128)(2,1)} custom-call(s32[16,28]{1,0:T(8,128)S(1)} %copy-done.14, bf16[2048,1024]{1,0:T(8,128)(2,1)} %bitcast.116, bf16[128,3584]{1,0:T(8,128)(2,1)S(1)} %get-tuple-element.46.refs_0_, bf16[128,3584]{1,0:T(8,128)(2,1)} %collective-permute-done.19.refs_1_, bf16[128,3584]{1,0:T(8,128)(2,1)} %collective-permute-done.20.refs_2_, ...), custom_call_target="tpu_custom_call" | custom-call | flops 15032385536 | bytes 22020096 | tf_op jit(solution)/shard_map/pallas_call | solution.py:125
  281.9 2.1 collective-permute-done.37.refs_6_
  284.0 20.7 %shard_map.121 = bf16[2048,3584]{1,0:T(8,128)(2,1)} custom-call(s32[16,28]{1,0:T(8,128)S(1)} %copy-done.15, bf16[2048,1024]{1,0:T(8,128)(2,1)} %bitcast.117, bf16[128,3584]{1,0:T(8,128)(2,1)S(1)} %get-tuple-element.45.refs_0_, bf16[128,3584]{1,0:T(8,128)(2,1)S(1)} %collective-permute-done.32.refs_1_, bf16[128,3584]{1,0:T(8,128)(2,1)S(1)} %collective-permute-done.33.refs_2_, ...), custom_call_target="tpu_custom_call" | custom-call | flops 15032385536 | bytes 22020096 | tf_op jit(solution)/shard_map/pallas_call | solution.py:125
  (177 shorter events, 46.5 us)
Async XLA Ops:
  15.3 9.5 %copy-start.8 = (bf16[512,2048]{1,0:T(8,128)(2,1)S(1)}, bf16[512,2048]{1,0:T(8,128)(2,1)}, u32[]{:S(2)}) copy-start(bf16[512,2048]{1,0:T(8,128)(2,1)} %x.4) | copy-start | bytes 6291460
  15.3 9.5 %copy-start.15 = (s32[16,28]{1,0:T(8,128)S(1)}, s32[16,28]{1,0:T(8,128)}, u32[]{:S(2)}) copy-start(s32[16,28]{1,0:T(8,128)} %keep.7) | copy-start | bytes 5380
  18.1 59.4 %collective-permute-start.1 = (bf16[2,64,3584]{2,1,0:T(8,128)(2,1)}, bf16[2,64,3584]{2,1,0:T(8,128)(2,1)}, u32[]{:S(2)}, u32[]{:S(2)}) collective-permute-start(bf16[2,64,3584]{2,1,0:T(8,128)(2,1)} %dynamic-slice_bitcast_fusion.5), channel_id=1, source_target_pairs={{0,4},{4,0},{8,12},{12,8},{1,5},{5,1},{9,13},{13,9},{2,6},{6,2},{1... | collective-permute-start | bytes 2752520 | tf_op jit(solution)/shard_map/ppermute | solution.py:212
  23.2 55.8 %collective-permute-start.3 = (bf16[2,64,3584]{2,1,0:T(8,128)(2,1)}, bf16[2,64,3584]{2,1,0:T(8,128)(2,1)}, u32[]{:S(2)}, u32[]{:S(2)}) collective-permute-start(bf16[2,64,3584]{2,1,0:T(8,128)(2,1)} %dynamic-slice_bitcast_fusion.4), channel_id=1, source_target_pairs={{0,8},{4,12},{8,0},{12,4},{1,9},{5,13},{9,1},{13,5},{2,10},{6,14},... | collective-permute-start | bytes 2752520 | tf_op jit(solution)/shard_map/ppermute | solution.py:212
  38.2 43.1 %collective-permute-start.5 = (bf16[2,64,3584]{2,1,0:T(8,128)(2,1)}, bf16[2,64,3584]{2,1,0:T(8,128)(2,1)}, u32[]{:S(2)}, u32[]{:S(2)}) collective-permute-start(bf16[2,64,3584]{2,1,0:T(8,128)(2,1)} %dynamic-slice_bitcast_fusion.3), channel_id=1, source_target_pairs={{0,4},{4,0},{8,12},{12,8},{1,5},{5,1},{9,13},{13,9},{2,6},{6,2},{1... | collective-permute-start | bytes 2752520 | tf_op jit(solution)/shard_map/ppermute | solution.py:212
  40.4 42.2 %collective-permute-start.7 = (bf16[2,64,3584]{2,1,0:T(8,128)(2,1)}, bf16[2,64,3584]{2,1,0:T(8,128)(2,1)}, u32[]{:S(2)}, u32[]{:S(2)}) collective-permute-start(bf16[2,64,3584]{2,1,0:T(8,128)(2,1)} %dynamic-slice_bitcast_fusion.2), channel_id=1, source_target_pairs={{0,8},{4,12},{8,0},{12,4},{1,9},{5,13},{9,1},{13,5},{2,10},{6,14},... | collective-permute-start | bytes 2752520 | tf_op jit(solution)/shard_map/ppermute | solution.py:212
  56.5 28.9 %collective-permute-start.12 = (bf16[2,64,3584]{2,1,0:T(8,128)(2,1)}, bf16[2,64,3584]{2,1,0:T(8,128)(2,1)}, u32[]{:S(2)}, u32[]{:S(2)}) collective-permute-start(bf16[2,64,3584]{2,1,0:T(8,128)(2,1)} %dynamic-slice_bitcast_fusion.1), channel_id=1, source_target_pairs={{0,4},{4,0},{8,12},{12,8},{1,5},{5,1},{9,13},{13,9},{2,6},{6,2},{1... | collective-permute-start | bytes 2752520 | tf_op jit(solution)/shard_map/ppermute | solution.py:212
  64.7 11.9 %copy-start.24 = (bf16[1,128,2048]{1,2,0:T(8,128)(2,1)}, bf16[1,128,2048]{1,2,0:T(8,128)(2,1)S(1)}, u32[]{:S(2)}) copy-start(bf16[1,128,2048]{1,2,0:T(8,128)(2,1)S(1)} %copy.82) | copy-start | bytes 1572868
  77.5 23.3 %collective-permute-start.14 = (bf16[2,64,3584]{2,1,0:T(8,128)(2,1)S(1)}, bf16[2,64,3584]{2,1,0:T(8,128)(2,1)S(1)}, u32[]{:S(2)}, u32[]{:S(2)}) collective-permute-start(bf16[2,64,3584]{2,1,0:T(8,128)(2,1)S(1)} %copy-done.32), channel_id=1, source_target_pairs={{0,8},{4,12},{8,0},{12,4},{1,9},{5,13},{9,1},{13,5},{2,10},{6,14},... | collective-permute-start | bytes 2752520 | tf_op jit(solution)/shard_map/ppermute | solution.py:212
  79.0 113.5 %collective-permute-start.23 = (bf16[512,2048]{1,0:T(8,128)(2,1)}, bf16[512,2048]{1,0:T(8,128)(2,1)}, u32[]{:S(2)}, u32[]{:S(2)}) collective-permute-start(bf16[512,2048]{1,0:T(8,128)(2,1)} %pad_maximum_fusion.4), channel_id=1, source_target_pairs={{0,16},{16,0},{1,17},{17,1},{2,18},{18,2},{3,19},{19,3},{4,20},{20... | collective-permute-start | bytes 6291464 | tf_op jit(solution)/shard_map/ppermute | solution.py:212
  81.3 22.8 %collective-permute-start.4 = (bf16[64,3584]{1,0:T(8,128)(2,1)S(1)}, bf16[64,3584]{1,0:T(8,128)(2,1)S(1)}, u32[]{:S(2)}, u32[]{:S(2)}) collective-permute-start(bf16[64,3584]{1,0:T(8,128)(2,1)S(1)} %fusion.7), channel_id=1, source_target_pairs={{0,4},{4,0},{8,12},{12,8},{1,5},{5,1},{9,13},{13,9},{2,6},{6,2},{1... | collective-permute-start | bytes 1376264 | tf_op jit(solution)/shard_map/ppermute | solution.py:212
  82.6 28.0 %collective-permute-start.2 = (bf16[64,3584]{1,0:T(8,128)(2,1)S(1)}, bf16[64,3584]{1,0:T(8,128)(2,1)S(1)}, u32[]{:S(2)}, u32[]{:S(2)}) collective-permute-start(bf16[64,3584]{1,0:T(8,128)(2,1)S(1)} %fusion.6), channel_id=1, source_target_pairs={{0,8},{4,12},{8,0},{12,4},{1,9},{5,13},{9,1},{13,5},{2,10},{6,14},... | collective-permute-start | bytes 1376264 | tf_op jit(solution)/shard_map/ppermute | solution.py:212
  83.1 19.2 %copy-start.3 = (bf16[512,3584]{1,0:T(8,128)(2,1)S(1)}, bf16[512,3584]{1,0:T(8,128)(2,1)}, u32[]{:S(2)}) copy-start(bf16[512,3584]{1,0:T(8,128)(2,1)} %copy-done.2) | copy-start | bytes 11010052
  85.4 26.9 %collective-permute-start.8 = (bf16[64,3584]{1,0:T(8,128)(2,1)S(1)}, bf16[64,3584]{1,0:T(8,128)(2,1)S(1)}, u32[]{:S(2)}, u32[]{:S(2)}) collective-permute-start(bf16[64,3584]{1,0:T(8,128)(2,1)S(1)} %fusion.9), channel_id=1, source_target_pairs={{0,4},{4,0},{8,12},{12,8},{1,5},{5,1},{9,13},{13,9},{2,6},{6,2},{1... | collective-permute-start | bytes 1376264 | tf_op jit(solution)/shard_map/ppermute | solution.py:212
  100.8 19.7 %collective-permute-start.6 = (bf16[64,3584]{1,0:T(8,128)(2,1)S(1)}, bf16[64,3584]{1,0:T(8,128)(2,1)S(1)}, u32[]{:S(2)}, u32[]{:S(2)}) collective-permute-start(bf16[64,3584]{1,0:T(8,128)(2,1)S(1)} %fusion.8), channel_id=1, source_target_pairs={{0,8},{4,12},{8,0},{12,4},{1,9},{5,13},{9,1},{13,5},{2,10},{6,14},... | collective-permute-start | bytes 1376264 | tf_op jit(solution)/shard_map/ppermute | solution.py:212
  104.2 21.8 %collective-permute-start.15 = (bf16[64,3584]{1,0:T(8,128)(2,1)S(1)}, bf16[64,3584]{1,0:T(8,128)(2,1)S(1)}, u32[]{:S(2)}, u32[]{:S(2)}) collective-permute-start(bf16[64,3584]{1,0:T(8,128)(2,1)S(1)} %fusion.11), channel_id=1, source_target_pairs={{0,4},{4,0},{8,12},{12,8},{1,5},{5,1},{9,13},{13,9},{2,6},{6,2},{1... | collective-permute-start | bytes 1376264 | tf_op jit(solution)/shard_map/ppermute | solution.py:212
  105.6 15.0 %copy-start.16 = (f32[64,3584]{1,0:T(8,128)}, f32[64,3584]{1,0:T(8,128)S(1)}, u32[]{:S(2)}) copy-start(f32[64,3584]{1,0:T(8,128)S(1)} %bitcast_add_fusion.4) | copy-start | bytes 2752516
  110.6 34.2 %collective-permute-start.13 = (bf16[64,3584]{1,0:T(8,128)(2,1)S(1)}, bf16[64,3584]{1,0:T(8,128)(2,1)S(1)}, u32[]{:S(2)}, u32[]{:S(2)}) collective-permute-start(bf16[64,3584]{1,0:T(8,128)(2,1)S(1)} %fusion.10), channel_id=1, source_target_pairs={{0,8},{4,12},{8,0},{12,4},{1,9},{5,13},{9,1},{13,5},{2,10},{6,14},... | collective-permute-start | bytes 1376264 | tf_op jit(solution)/shard_map/ppermute | solution.py:212
  122.3 9.6 %collective-permute-start.11 = (bf16[7,128,128]{2,1,0:T(8,128)(2,1)S(1)}, bf16[7,128,128]{2,1,0:T(8,128)(2,1)S(1)}, u32[]{:S(2)}, u32[]{:S(2)}) collective-permute-start(bf16[7,128,128]{2,1,0:T(8,128)(2,1)S(1)} %get-tuple-element.55), channel_id=1, source_target_pairs={{0,3},{1,2},{2,1},{3,0},{4,7},{5,6},{6,5},{7,4},{8,11},{9,10},{10,... | collective-permute-start | bytes 688136 | tf_op jit(solution)/shard_map/ppermute | solution.py:212
  126.0 14.7 %collective-permute-start.10 = (bf16[7,128,128]{2,1,0:T(8,128)(2,1)S(1)}, bf16[7,128,128]{2,1,0:T(8,128)(2,1)S(1)}, u32[]{:S(2)}, u32[]{:S(2)}) collective-permute-start(bf16[7,128,128]{2,1,0:T(8,128)(2,1)S(1)} %get-tuple-element.56), channel_id=1, source_target_pairs={{0,2},{1,3},{2,0},{3,1},{4,6},{5,7},{6,4},{7,5},{8,10},{9,11},{10,... | collective-permute-start | bytes 688136 | tf_op jit(solution)/shard_map/ppermute | solution.py:212
  126.0 14.7 %collective-permute-start.9 = (bf16[7,128,128]{2,1,0:T(8,128)(2,1)S(1)}, bf16[7,128,128]{2,1,0:T(8,128)(2,1)S(1)}, u32[]{:S(2)}, u32[]{:S(2)}) collective-permute-start(bf16[7,128,128]{2,1,0:T(8,128)(2,1)S(1)} %get-tuple-element.57), channel_id=1, source_target_pairs={{0,1},{1,0},{2,3},{3,2},{4,5},{5,4},{6,7},{7,6},{8,9},{9,8},{10,11... | collective-permute-start | bytes 688136 | tf_op jit(solution)/shard_map/ppermute | solution.py:212
  141.4 21.3 %collective-permute-start.25 = (bf16[128,3584]{1,0:T(8,128)(2,1)S(1)}, bf16[128,3584]{1,0:T(8,128)(2,1)S(1)}, u32[]{:S(2)}, u32[]{:S(2)}) collective-permute-start(bf16[128,3584]{1,0:T(8,128)(2,1)S(1)} %shard_map.116.refs_0_), channel_id=1, source_target_pairs={{0,8},{4,12},{8,0},{12,4},{1,9},{5,13},{9,1},{13,5},{2,10},{6,14},... | collective-permute-start | bytes 2752520 | tf_op jit(solution)/shard_map/ppermute | solution.py:212
  143.0 21.2 %collective-permute-start.24 = (bf16[128,3584]{1,0:T(8,128)(2,1)S(1)}, bf16[128,3584]{1,0:T(8,128)(2,1)}, u32[]{:S(2)}, u32[]{:S(2)}) collective-permute-start(bf16[128,3584]{1,0:T(8,128)(2,1)S(1)} %shard_map.116.refs_0_), channel_id=1, source_target_pairs={{0,4},{4,0},{8,12},{12,8},{1,5},{5,1},{9,13},{13,9},{2,6},{6,2},{1... | collective-permute-start | bytes 2752520 | tf_op jit(solution)/shard_map/ppermute | solution.py:212
  148.6 20.5 %collective-permute-start.18 = (bf16[7,128,128]{2,1,0:T(8,128)(2,1)}, bf16[7,128,128]{2,1,0:T(8,128)(2,1)S(1)}, u32[]{:S(2)}, u32[]{:S(2)}) collective-permute-start(bf16[7,128,128]{2,1,0:T(8,128)(2,1)} %get-tuple-element.51), channel_id=1, source_target_pairs={{0,3},{1,2},{2,1},{3,0},{4,7},{5,6},{6,5},{7,4},{8,11},{9,10},{10,... | collective-permute-start | bytes 688136 | tf_op jit(solution)/shard_map/ppermute | solution.py:212
  151.0 18.1 %collective-permute-start.17 = (bf16[7,128,128]{2,1,0:T(8,128)(2,1)}, bf16[7,128,128]{2,1,0:T(8,128)(2,1)S(1)}, u32[]{:S(2)}, u32[]{:S(2)}) collective-permute-start(bf16[7,128,128]{2,1,0:T(8,128)(2,1)} %get-tuple-element.52), channel_id=1, source_target_pairs={{0,2},{1,3},{2,0},{3,1},{4,6},{5,7},{6,4},{7,5},{8,10},{9,11},{10,... | collective-permute-start | bytes 688136 | tf_op jit(solution)/shard_map/ppermute | solution.py:212
  162.8 10.4 %copy-start.9 = (bf16[128,3584]{1,0:T(8,128)(2,1)}, bf16[128,3584]{1,0:T(8,128)(2,1)S(1)}, u32[]{:S(2)}) copy-start(bf16[128,3584]{1,0:T(8,128)(2,1)S(1)} %collective-permute-done.25.refs_2_) | copy-start | bytes 2752516
  162.8 9.6 %collective-permute-start.16 = (bf16[7,128,128]{2,1,0:T(8,128)(2,1)S(1)}, bf16[7,128,128]{2,1,0:T(8,128)(2,1)S(1)}, u32[]{:S(2)}, u32[]{:S(2)}) collective-permute-start(bf16[7,128,128]{2,1,0:T(8,128)(2,1)S(1)} %get-tuple-element.53), channel_id=1, source_target_pairs={{0,1},{1,0},{2,3},{3,2},{4,5},{5,4},{6,7},{7,6},{8,9},{9,8},{10,11... | collective-permute-start | bytes 688136 | tf_op jit(solution)/shard_map/ppermute | solution.py:212
  167.1 46.3 %collective-permute-start.28 = (bf16[384,3584]{1,0:T(8,128)(2,1)}, bf16[384,3584]{1,0:T(8,128)(2,1)}, u32[]{:S(2)}, u32[]{:S(2)}) collective-permute-start(bf16[384,3584]{1,0:T(8,128)(2,1)} %pad_maximum_fusion), channel_id=1, source_target_pairs={{0,16},{16,0},{1,17},{17,1},{2,18},{18,2},{3,19},{19,3},{4,20},{20... | collective-permute-start | bytes 8257544 | tf_op jit(solution)/shard_map/ppermute | solution.py:212
  173.2 11.5 %collective-permute-start.27 = (bf16[64,3584]{1,0:T(8,128)(2,1)S(1)}, bf16[64,3584]{1,0:T(8,128)(2,1)S(1)}, u32[]{:S(2)}, u32[]{:S(2)}) collective-permute-start(bf16[64,3584]{1,0:T(8,128)(2,1)S(1)} %slice.67), channel_id=1, source_target_pairs={{0,4},{4,0},{8,12},{12,8},{1,5},{5,1},{9,13},{13,9},{2,6},{6,2},{1... | collective-permute-start | bytes 1376264 | tf_op jit(solution)/shard_map/ppermute | solution.py:212
  175.5 13.5 %collective-permute-start.26 = (bf16[64,3584]{1,0:T(8,128)(2,1)S(1)}, bf16[64,3584]{1,0:T(8,128)(2,1)S(1)}, u32[]{:S(2)}, u32[]{:S(2)}) collective-permute-start(bf16[64,3584]{1,0:T(8,128)(2,1)S(1)} %slice.66), channel_id=1, source_target_pairs={{0,8},{4,12},{8,0},{12,4},{1,9},{5,13},{9,1},{13,5},{2,10},{6,14},... | collective-permute-start | bytes 1376264 | tf_op jit(solution)/shard_map/ppermute | solution.py:212
  176.4 14.5 %copy-start.31 = (bf16[1,128,2048]{1,2,0:T(8,128)(2,1)S(1)}, bf16[1,128,2048]{1,2,0:T(8,128)(2,1)}, u32[]{:S(2)}) copy-start(bf16[1,128,2048]{1,2,0:T(8,128)(2,1)} %copy.83) | copy-start | bytes 1572868
  177.6 13.2 %copy-start.25 = (bf16[1,128,2048]{1,2,0:T(8,128)(2,1)S(1)}, bf16[1,128,2048]{1,2,0:T(8,128)(2,1)}, u32[]{:S(2)}) copy-start(bf16[1,128,2048]{1,2,0:T(8,128)(2,1)} %copy-done.24) | copy-start | bytes 1572868
  177.6 13.2 %copy-start.27 = (bf16[1,128,2048]{1,2,0:T(8,128)(2,1)S(1)}, bf16[1,128,2048]{1,2,0:T(8,128)(2,1)}, u32[]{:S(2)}) copy-start(bf16[1,128,2048]{1,2,0:T(8,128)(2,1)} %copy.81) | copy-start | bytes 1572868
  177.6 13.2 %copy-start.28 = (bf16[1,128,2048]{1,2,0:T(8,128)(2,1)S(1)}, bf16[1,128,2048]{1,2,0:T(8,128)(2,1)}, u32[]{:S(2)}) copy-start(bf16[1,128,2048]{1,2,0:T(8,128)(2,1)} %copy.84) | copy-start | bytes 1572868
  177.6 29.5 %collective-permute-start.20 = (bf16[128,3584]{1,0:T(8,128)(2,1)S(1)}, bf16[128,3584]{1,0:T(8,128)(2,1)}, u32[]{:S(2)}, u32[]{:S(2)}) collective-permute-start(bf16[128,3584]{1,0:T(8,128)(2,1)S(1)} %get-tuple-element.46.refs_0_), channel_id=1, source_target_pairs={{0,8},{4,12},{8,0},{12,4},{1,9},{5,13},{9,1},{13,5},{2,10},{6,14},... | collective-permute-start | bytes 2752520 | tf_op jit(solution)/shard_map/ppermute | solution.py:212
  184.8 24.4 %collective-permute-start.19 = (bf16[128,3584]{1,0:T(8,128)(2,1)S(1)}, bf16[128,3584]{1,0:T(8,128)(2,1)}, u32[]{:S(2)}, u32[]{:S(2)}) collective-permute-start(bf16[128,3584]{1,0:T(8,128)(2,1)S(1)} %get-tuple-element.46.refs_0_), channel_id=1, source_target_pairs={{0,4},{4,0},{8,12},{12,8},{1,5},{5,1},{9,13},{13,9},{2,6},{6,2},{1... | collective-permute-start | bytes 2752520 | tf_op jit(solution)/shard_map/ppermute | solution.py:212
  190.8 21.8 %collective-permute-start.29 = (bf16[128,3584]{1,0:T(8,128)(2,1)}, bf16[128,3584]{1,0:T(8,128)(2,1)}, u32[]{:S(2)}, u32[]{:S(2)}) collective-permute-start(bf16[128,3584]{1,0:T(8,128)(2,1)} %pad_maximum_fusion.8), channel_id=1, source_target_pairs={{0,16},{16,0},{1,17},{17,1},{2,18},{18,2},{3,19},{19,3},{4,20},{20... | collective-permute-start | bytes 2752520 | tf_op jit(solution)/shard_map/ppermute | solution.py:212
  192.5 46.1 %collective-permute-start = (bf16[512,2048]{0,1:T(8,128)(2,1)}, bf16[512,2048]{0,1:T(8,128)(2,1)S(1)}, u32[]{:S(2)}, u32[]{:S(2)}) collective-permute-start(bf16[512,2048]{0,1:T(8,128)(2,1)} %pad_maximum_fusion.3), channel_id=1, source_target_pairs={{0,16},{16,0},{1,17},{17,1},{2,18},{18,2},{3,19},{19,3},{4,20},{20... | collective-permute-start | bytes 6291464 | tf_op jit(solution)/shard_map/ppermute | solution.py:212
  207.1 33.1 %collective-permute-start.33 = (bf16[128,3584]{1,0:T(8,128)(2,1)S(1)}, bf16[128,3584]{1,0:T(8,128)(2,1)S(1)}, u32[]{:S(2)}, u32[]{:S(2)}) collective-permute-start(bf16[128,3584]{1,0:T(8,128)(2,1)S(1)} %get-tuple-element.45.refs_0_), channel_id=1, source_target_pairs={{0,8},{4,12},{8,0},{12,4},{1,9},{5,13},{9,1},{13,5},{2,10},{6,14},... | collective-permute-start | bytes 2752520 | tf_op jit(solution)/shard_map/ppermute | solution.py:212
  209.2 25.3 %collective-permute-start.22 = (bf16[64,3584]{1,0:T(8,128)(2,1)S(1)}, bf16[64,3584]{1,0:T(8,128)(2,1)S(1)}, u32[]{:S(2)}, u32[]{:S(2)}) collective-permute-start(bf16[64,3584]{1,0:T(8,128)(2,1)S(1)} %slice.65), channel_id=1, source_target_pairs={{0,4},{4,0},{8,12},{12,8},{1,5},{5,1},{9,13},{13,9},{2,6},{6,2},{1... | collective-permute-start | bytes 1376264 | tf_op jit(solution)/shard_map/ppermute | solution.py:212
  212.6 25.0 %collective-permute-start.21 = (bf16[64,3584]{1,0:T(8,128)(2,1)S(1)}, bf16[64,3584]{1,0:T(8,128)(2,1)S(1)}, u32[]{:S(2)}, u32[]{:S(2)}) collective-permute-start(bf16[64,3584]{1,0:T(8,128)(2,1)S(1)} %slice.64), channel_id=1, source_target_pairs={{0,8},{4,12},{8,0},{12,4},{1,9},{5,13},{9,1},{13,5},{2,10},{6,14},... | collective-permute-start | bytes 1376264 | tf_op jit(solution)/shard_map/ppermute | solution.py:212
  213.4 47.1 %collective-permute-start.30 = (bf16[384,3584]{1,0:T(8,128)(2,1)S(1)}, bf16[384,3584]{1,0:T(8,128)(2,1)}, u32[]{:S(2)}, u32[]{:S(2)}) collective-permute-start(bf16[384,3584]{1,0:T(8,128)(2,1)S(1)} %pad_maximum_fusion.1), channel_id=1, source_target_pairs={{0,16},{16,0},{1,17},{17,1},{2,18},{18,2},{3,19},{19,3},{4,20},{20... | collective-permute-start | bytes 8257544 | tf_op jit(solution)/shard_map/ppermute | solution.py:212
  234.5 22.8 %collective-permute-start.32 = (bf16[128,3584]{1,0:T(8,128)(2,1)S(1)}, bf16[128,3584]{1,0:T(8,128)(2,1)S(1)}, u32[]{:S(2)}, u32[]{:S(2)}) collective-permute-start(bf16[128,3584]{1,0:T(8,128)(2,1)S(1)} %get-tuple-element.45.refs_0_), channel_id=1, source_target_pairs={{0,4},{4,0},{8,12},{12,8},{1,5},{5,1},{9,13},{13,9},{2,6},{6,2},{1... | collective-permute-start | bytes 2752520 | tf_op jit(solution)/shard_map/ppermute | solution.py:212
  237.7 22.8 %collective-permute-start.31 = (bf16[128,3584]{1,0:T(8,128)(2,1)S(1)}, bf16[128,3584]{1,0:T(8,128)(2,1)S(1)}, u32[]{:S(2)}, u32[]{:S(2)}) collective-permute-start(bf16[128,3584]{1,0:T(8,128)(2,1)S(1)} %pad_maximum_fusion.9), channel_id=1, source_target_pairs={{0,16},{16,0},{1,17},{17,1},{2,18},{18,2},{3,19},{19,3},{4,20},{20... | collective-permute-start | bytes 2752520 | tf_op jit(solution)/shard_map/ppermute | solution.py:212
  257.4 23.8 %collective-permute-start.35 = (bf16[64,3584]{1,0:T(8,128)(2,1)S(1)}, bf16[64,3584]{1,0:T(8,128)(2,1)S(1)}, u32[]{:S(2)}, u32[]{:S(2)}) collective-permute-start(bf16[64,3584]{1,0:T(8,128)(2,1)S(1)} %slice.55), channel_id=1, source_target_pairs={{0,4},{4,0},{8,12},{12,8},{1,5},{5,1},{9,13},{13,9},{2,6},{6,2},{1... | collective-permute-start | bytes 1376264 | tf_op jit(solution)/shard_map/ppermute | solution.py:212
  259.2 22.0 %collective-permute-start.34 = (bf16[64,3584]{1,0:T(8,128)(2,1)S(1)}, bf16[64,3584]{1,0:T(8,128)(2,1)S(1)}, u32[]{:S(2)}, u32[]{:S(2)}) collective-permute-start(bf16[64,3584]{1,0:T(8,128)(2,1)S(1)} %slice.54), channel_id=1, source_target_pairs={{0,8},{4,12},{8,0},{12,4},{1,9},{5,13},{9,1},{13,5},{2,10},{6,14},... | collective-permute-start | bytes 1376264 | tf_op jit(solution)/shard_map/ppermute | solution.py:212
  260.4 23.5 %collective-permute-start.36 = (bf16[384,3584]{1,0:T(8,128)(2,1)S(1)}, bf16[384,3584]{1,0:T(8,128)(2,1)}, u32[]{:S(2)}, u32[]{:S(2)}) collective-permute-start(bf16[384,3584]{1,0:T(8,128)(2,1)S(1)} %pad_maximum_fusion.2), channel_id=1, source_target_pairs={{0,16},{16,0},{1,17},{17,1},{2,18},{18,2},{3,19},{19,3},{4,20},{20... | collective-permute-start | bytes 8257544 | tf_op jit(solution)/shard_map/ppermute | solution.py:212
  281.3 2.6 collective-permute-start.37
  (25 other events, 101.3 us)
